TPU v7x, 32 devices: a whole 2x2x4 slice. The times are simulated.
32 devices in a mesh: ctx: 16 (over z, y, core), head: 2 (over x).
Axes of the slice: x: 2, y: 2, z: 4, core: 2. Of those that a mesh axis runs over, the one named last changes fastest.
Arguments:
- queries: bfloat16 [2048, 4096], P(('ctx', 'head')), may hold values from -4.6 to 4.6
- key_states: bfloat16 [2048, 4096], P(('ctx', 'head')), may hold values from -4.6 to 4.6
- value_states: bfloat16 [2048, 4096], P(('ctx', 'head')), may hold values from -6 to 6
- out_grad: bfloat16 [2048, 4096], P(('ctx', 'head')), may hold values from -6 to 6
- random_blocks: int32 [64, 3], replicated, may hold values from 0 to 63, as said below
- global_blocks: int32 [4], replicated, may hold values from 0 to 63, as said below
Outputs:
- query_grad: bfloat16 [2048, 4096], P('ctx', 'head')
- key_grad: bfloat16 [2048, 4096], P('ctx', 'head')
- value_grad: bfloat16 [2048, 4096], P('ctx', 'head')
Inputs may be any that keep to these rules, and one draw needn't show every extreme that they name: `random_blocks`: with the blocks i * 4 to i * 4 + 3 called range i: the 12 entries of the rows of range i name blocks of any one range at most 1 times, and some range exactly 1 times. `global_blocks`: 4 different blocks, one of them the last block 63, in any order.
All inputs are finite; a program needn't handle non-finite values.
Results may differ from a plain program's by a relative error of at most 0.0077.
Values may be sent and summed in bfloat16 or wider, within the bound.
A program may use at most 128 MiB of HBM per device.

v0:
```python
import math

import jax
import jax.numpy as jnp
from jax import lax
from jax.sharding import PartitionSpec as P

DH = 128
BS = 32
NR = 3
NG = 4


def with_halo(x, sides, width):
    for axis, dim in sides:
        peers, length = (lax.axis_size(axis), x.shape[dim])
        up = [(i, (i + 1) % peers) for i in range(peers - 1)]
        down = [(j, i) for i, j in up]
        last = lax.slice_in_dim(x, length - width, length, axis=dim)
        first = lax.slice_in_dim(x, 0, width, axis=dim)
        before = lax.ppermute(last, axis, up)
        after = lax.ppermute(first, axis, down)
        x = jnp.concatenate([before, x, after], axis=dim)
    return x


def spread(x, axis, root):
    mine = lax.axis_index(axis) == root
    return lax.psum(jnp.where(mine, x, jnp.zeros_like(x)), axis)


def per_device(queries, key_states, value_states, out_grad, random_blocks, global_blocks):
    query_rows, key_rows, value_rows, grad_rows = (
        lax.all_to_all(queries, "head", split_axis=1, concat_axis=0, tiled=True),
        lax.all_to_all(key_states, "head", split_axis=1, concat_axis=0, tiled=True),
        lax.all_to_all(value_states, "head", split_axis=1, concat_axis=0, tiled=True),
        lax.all_to_all(out_grad, "head", split_axis=1, concat_axis=0, tiled=True),
    )
    tokens = query_rows.shape[0]
    head_cols = query_rows.shape[1]
    heads_here = head_cols // DH
    blocks_here = tokens // BS
    devices = lax.axis_size("ctx")
    my_index = lax.axis_index("ctx")
    total_blocks = devices * blocks_here
    entries = blocks_here * NR
    capacity = (entries + devices - 1) // devices
    inv_root = 1.0 / math.sqrt(DH)
    kv_rows = jnp.concatenate([key_rows, value_rows], axis=1)
    kv_blocks = kv_rows.reshape(blocks_here, BS, 2 * head_cols)
    extended = with_halo(kv_rows, (("ctx", 0),), BS)
    extended = extended.reshape(blocks_here + 2, BS, 2 * head_cols)
    window = jnp.stack(
        [extended[:blocks_here], extended[1 : blocks_here + 1], extended[2:]], axis=1
    )
    global_owner = global_blocks // blocks_here
    global_offset = global_blocks % blocks_here
    pieces = []
    for member in range(NG):
        own_block = lax.dynamic_index_in_dim(kv_blocks, global_offset[member], 0, keepdims=False)
        pieces.append(spread(own_block, "ctx", global_owner[member]))
    global_kv = jnp.stack(pieces)
    entry_table = random_blocks.reshape(devices, entries)
    table_owner = entry_table // blocks_here
    table_offset = entry_table % blocks_here
    positions = jnp.arange(entries, dtype=jnp.int32)
    before = positions[None, :] < positions[:, None]
    matches = (table_owner[:, :, None] == table_owner[:, None, :]) & before[None]
    table_slot = jnp.sum(matches.astype(jnp.int32), axis=2)
    my_owner = lax.dynamic_index_in_dim(table_owner, my_index, 0, keepdims=False)
    my_slot = lax.dynamic_index_in_dim(table_slot, my_index, 0, keepdims=False)
    my_target = my_owner * capacity + my_slot
    slot_ids = jnp.arange(capacity, dtype=jnp.int32)
    served = (table_owner == my_index)[:, :, None] & (
        table_slot[:, :, None] == slot_ids[None, None, :]
    )
    served_block = jnp.sum(jnp.where(served, table_offset[:, :, None], 0), axis=1).reshape(-1)
    served_used = jnp.any(served, axis=1).reshape(-1)
    outgoing = jnp.take(kv_blocks, served_block, axis=0)
    incoming = lax.all_to_all(outgoing, "ctx", split_axis=0, concat_axis=0, tiled=True)
    fetched = jnp.take(incoming, my_target, axis=0).reshape(blocks_here, NR, BS, 2 * head_cols)
    near_kv = jnp.concatenate([window, fetched], axis=1)
    near_groups = 3 + NR
    near_count = near_groups * BS
    query_heads = query_rows.reshape(blocks_here, BS, heads_here, DH)
    grad_heads = grad_rows.reshape(blocks_here, BS, heads_here, DH)
    near_keys = near_kv[..., :head_cols].reshape(blocks_here, near_groups, BS, heads_here, DH)
    near_values = near_kv[..., head_cols:].reshape(blocks_here, near_groups, BS, heads_here, DH)
    far_keys = global_kv[..., :head_cols].reshape(NG, BS, heads_here, DH)
    far_values = global_kv[..., head_cols:].reshape(NG, BS, heads_here, DH)
    scores = (
        jnp.concatenate(
            [
                jnp.einsum(
                    "bqhd,bgkhd->bhqgk", query_heads, near_keys, preferred_element_type=jnp.float32
                ).reshape(blocks_here, heads_here, BS, near_count),
                jnp.einsum(
                    "bqhd,gkhd->bhqgk", query_heads, far_keys, preferred_element_type=jnp.float32
                ).reshape(blocks_here, heads_here, BS, NG * BS),
            ],
            axis=3,
        )
        * inv_root
    )
    block_ids = my_index * blocks_here + jnp.arange(blocks_here, dtype=jnp.int32)
    usable = jnp.concatenate(
        [
            (block_ids > 0)[:, None],
            jnp.ones((blocks_here, 1), bool),
            (block_ids < total_blocks - 1)[:, None],
            jnp.ones((blocks_here, NR + NG), bool),
        ],
        axis=1,
    )
    column_ok = jnp.repeat(usable, BS, axis=1)[:, None, None, :]
    masked = jnp.where(column_ok, scores, -jnp.inf)
    row_max = jnp.max(masked, axis=3, keepdims=True)
    log_total = row_max + jnp.log(jnp.sum(jnp.exp(masked - row_max), axis=3, keepdims=True))
    probs_full = jnp.exp(masked - log_total)
    probs_half = probs_full.astype(jnp.bfloat16)
    near_probs = probs_half[..., :near_count].reshape(blocks_here, heads_here, BS, near_groups, BS)
    far_probs = probs_half[..., near_count:].reshape(blocks_here, heads_here, BS, NG, BS)
    outputs = jnp.einsum(
        "bhqgk,bgkhd->bqhd", near_probs, near_values, preferred_element_type=jnp.float32
    ) + jnp.einsum("bhqgk,gkhd->bqhd", far_probs, far_values, preferred_element_type=jnp.float32)
    row_dot = jnp.sum(grad_heads.astype(jnp.float32) * outputs, axis=3)
    dprobs = jnp.concatenate(
        [
            jnp.einsum(
                "bqhd,bgkhd->bhqgk", grad_heads, near_values, preferred_element_type=jnp.float32
            ).reshape(blocks_here, heads_here, BS, near_count),
            jnp.einsum(
                "bqhd,gkhd->bhqgk", grad_heads, far_values, preferred_element_type=jnp.float32
            ).reshape(blocks_here, heads_here, BS, NG * BS),
        ],
        axis=3,
    )
    dscores = probs_full * (dprobs - jnp.transpose(row_dot, (0, 2, 1))[..., None])
    ds_half = dscores.astype(jnp.bfloat16)
    near_ds = ds_half[..., :near_count].reshape(blocks_here, heads_here, BS, near_groups, BS)
    far_ds = ds_half[..., near_count:].reshape(blocks_here, heads_here, BS, NG, BS)
    query_grad = (
        (
            (
                jnp.einsum(
                    "bhqgk,bgkhd->bqhd", near_ds, near_keys, preferred_element_type=jnp.float32
                )
                + jnp.einsum(
                    "bhqgk,gkhd->bqhd", far_ds, far_keys, preferred_element_type=jnp.float32
                )
            )
            * inv_root
        )
        .astype(jnp.bfloat16)
        .reshape(tokens, head_cols)
    )

    def key_value_parts(ds_part, probs_part):
        key_part = (
            jnp.einsum(
                "bhqgk,bqhd->bgkhd", ds_part, query_heads, preferred_element_type=jnp.float32
            )
            * inv_root
        )
        value_part = jnp.einsum(
            "bhqgk,bqhd->bgkhd", probs_part, grad_heads, preferred_element_type=jnp.float32
        )
        out_shape = key_part.shape[:3] + (head_cols,)
        return jnp.concatenate([key_part.reshape(out_shape), value_part.reshape(out_shape)], axis=3)

    random_part = key_value_parts(near_ds[:, :, :, 3:], near_probs[:, :, :, 3:])
    random_part = random_part.astype(jnp.bfloat16).reshape(entries, BS, 2 * head_cols)
    back_rows = (
        jnp.zeros((devices * capacity, BS, 2 * head_cols), jnp.bfloat16)
        .at[my_target]
        .set(random_part)
    )
    arrived = lax.all_to_all(back_rows, "ctx", split_axis=0, concat_axis=0, tiled=True)
    window_part = key_value_parts(near_ds[:, :, :, :3], near_probs[:, :, :, :3])
    zero_block = jnp.zeros((1, BS, 2 * head_cols), jnp.float32)
    own_grad = (
        window_part[:, 1]
        + jnp.concatenate([window_part[1:, 0], zero_block], axis=0)
        + jnp.concatenate([zero_block, window_part[:-1, 2]], axis=0)
    )
    rims_out = jnp.concatenate([window_part[0, 0], window_part[blocks_here - 1, 2]], axis=0)
    rims_in = with_halo(rims_out.astype(jnp.bfloat16), (("ctx", 0),), BS).astype(rims_out.dtype)
    own_grad = own_grad.at[0].add(rims_in[:BS]).at[blocks_here - 1].add(rims_in[3 * BS :])
    far_key = (
        jnp.einsum("bhqgk,bqhd->gkhd", far_ds, query_heads, preferred_element_type=jnp.float32)
        * inv_root
    )
    far_value = jnp.einsum(
        "bhqgk,bqhd->gkhd", far_probs, grad_heads, preferred_element_type=jnp.float32
    )
    far_part = jnp.concatenate(
        [far_key.reshape(NG, BS, head_cols), far_value.reshape(NG, BS, head_cols)], axis=2
    )
    far_sum = lax.psum(far_part, "ctx")
    here_ids = jnp.arange(blocks_here, dtype=jnp.int32)
    own_global = (
        (global_owner == my_index)[None, :] & (global_offset[None, :] == here_ids[:, None])
    ).astype(jnp.float32)
    own_grad = own_grad + jnp.einsum(
        "jg,gkc->jkc", own_global, far_sum, precision=lax.Precision.HIGHEST
    )
    weights = (served_used[None, :] & (served_block[None, :] == here_ids[:, None])).astype(
        jnp.bfloat16
    )
    own_grad = own_grad + jnp.einsum(
        "jr,rkc->jkc", weights, arrived, preferred_element_type=jnp.float32
    )
    key_grad = own_grad[..., :head_cols].astype(jnp.bfloat16).reshape(tokens, head_cols)
    value_grad = own_grad[..., head_cols:].astype(jnp.bfloat16).reshape(tokens, head_cols)
    return (query_grad, key_grad, value_grad)


def solution(mesh):
    placed = (
        P(("ctx", "head"), None),
        P(("ctx", "head"), None),
        P(("ctx", "head"), None),
        P(("ctx", "head"), None),
        P(),
        P(),
    )
    return jax.shard_map(
        per_device,
        mesh=mesh,
        in_specs=placed,
        out_specs=(P("ctx", "head"), P("ctx", "head"), P("ctx", "head")),
        check_vma=False,
    )
```

profile of v0, /device:TPU:13, one launch (start us, length us, event | category | flops | bytes accessed | tf_op | source)
XLA Modules:
  0.0 553.7 jit_solution(8503003226122069492)
XLA Ops:
  7.2 2.0 copy.536
  9.2 3.5 all-to-all-start.1
  16.6 3.4 all-to-all-done.1
  20.0 3.5 all-to-all-start
  25.2 4.8 all-to-all-done
  30.0 3.5 all-to-all-start.4
  33.6 2.8 gather_fusion
  36.3 2.6 all-to-all-done.4
  38.9 3.5 all-to-all-start.3
  42.4 4.6 broadcast_select_fusion
  47.8 10.6 %all-to-all-start.2 = ((bf16[16,32,4096]{2,1,0:T(8,128)(2,1)}), bf16[16,32,4096]{2,1,0:T(8,128)(2,1)}, u32[]{:S(2)}, u32[]{:S(2)}) async-start(bf16[16,32,4096]{2,1,0:T(8,128)(2,1)} %broadcast_select_fusion), calls=%async_computation.2 | async-start | bytes 8388608 | tf_op jit(solution)/shard_map/all_to_all | solution.py:80
  71.0 3.3 collective-permute-start
  74.4 2.2 collective-permute-start.1
  79.8 79.3 %collective-permute-done = bf16[32,4096]{1,0:T(8,128)(2,1)S(1)} collective-permute-done((bf16[32,4096]{1,0:T(8,128)(2,1)S(1)}, bf16[32,4096]{1,0:T(8,128)(2,1)S(1)}, u32[]{:S(2)}, u32[]{:S(2)}) %collective-permute-start) | collective-permute-done | bytes 262176 | tf_op jit(solution)/shard_map/ppermute | solution.py:21
  159.1 2.0 collective-permute-done.1
  161.1 2.2 pad_maximum_fusion.6
  163.3 51.6 %all-reduce.8.cloned.1.call-done = (bf16[1,32,4096]{2,1,0:T(8,128)(2,1)}, bf16[1,32,4096]{2,1,0:T(8,128)(2,1)}, bf16[1,32,4096]{2,1,0:T(8,128)(2,1)}, bf16[1,32,4096]{2,1,0:T(8,128)(2,1)}) async-done(((bf16[1,32,4096]{2,1,0:T(8,128)(2,1)}, bf16[1,32,4096]{2,1,0:T(8,128)(2,1)}, bf16[1,32,4096]{2,1,0:T(8,128)(2,1)}, bf16[1,32,4096]{2,1,0:T(8,128)(2,1)}), (bf16[1,32,4096]{2,1,0:T(8,128)(2,1)}, ...) | async-done | bytes 1048592 | tf_op jit(solution)/shard_map/psum | solution.py:29
  221.3 2.9 convolution_bitcast_fusion
  224.2 5.4 copy.312
  229.6 4.6 reshape.369
  234.5 3.0 convolution_bitcast_fusion.1
  237.5 5.3 copy.305
  242.8 3.7 reshape.364
  246.5 4.7 gather_fusion.1
  251.2 2.4 broadcast_select_fusion.1
  254.8 3.7 slice_bitcast_fusion
  258.5 3.6 fusion.6
  262.1 5.4 copy.306
  273.5 3.6 fusion.4
  277.1 5.9 %copy.313 = f32[4,16,32,192]{3,2,1,0:T(8,128)} copy(f32[4,16,32,192]{2,3,1,0:T(8,128)} %bitcast.260) | data formatting | bytes 3145728 | tf_op jit(solution)/shard_map/reshape | solution.py:131
  283.0 5.5 reshape.370
  288.5 5.7 %fusion.57 = f32[4,32,16,128]{3,1,2,0:T(8,128)} fusion(bf16[4,6,4,16,8,128]{5,4,3,2,1,0:T(8,128)(2,1)} %get-tuple-element.37, bf16[4,16,32,6,32]{4,3,2,1,0:T(8,128)(2,1)} %reshape.370), kind=kOutput, calls=%fused_computation.75 | convolution fusion | flops 100663296 | bytes 4980736 | tf_op jit(solution)/shard_map/bhqgk,bgkhd->bqhd/dot_general | solution.py:123
  294.1 4.0 reshape.371
  298.1 3.3 fusion.83
  301.4 2.2 fusion.12
  305.8 5.8 %reshape.372 = bf16[4,16,32,6,32]{4,3,2,1,0:T(8,128)(2,1)} reshape(bf16[4,16,32,192]{3,2,1,0:T(8,128)(2,1)} %slice.200) | data formatting | bytes 1572864 | tf_op jit(solution)/shard_map/reshape | solution.py:140
  311.7 4.8 fusion.52
  316.4 3.8 fusion.136
  320.2 3.7 fusion.137
  324.8 4.0 multiply_bitcast_fusion
  331.4 3.7 concatenate.86
  335.1 2.3 fusion.37
  339.2 3.7 concatenate.85
  342.9 3.9 pad_maximum_fusion.1
  346.8 2.5 broadcast_in_dim.69
  349.3 8.3 %scatter_fusion = bf16[16,32,4096]{2,1,0:T(8,128)(2,1)} fusion(bf16[16,32,4096]{2,1,0:T(8,128)(2,1)} %broadcast_in_dim.69, s32[12]{0:T(128)S(1)} %fusion.133, bf16[12,32,4096]{2,1,0:T(8,128)(2,1)} %pad_maximum_fusion.1), kind=kCustom, calls=%fused_computation.2 | custom fusion | bytes 9437232 | tf_op jit(solution)/shard_map/scatter | solution.py:176
  357.7 7.5 %all-to-all-start.5 = ((bf16[16,32,4096]{2,1,0:T(8,128)(2,1)}), bf16[16,32,4096]{2,1,0:T(8,128)(2,1)}, u32[]{:S(2)}, u32[]{:S(2)}) async-start(bf16[16,32,4096]{2,1,0:T(8,128)(2,1)} %scatter_fusion), calls=%async_computation.5 | async-start | bytes 8388608 | tf_op jit(solution)/shard_map/all_to_all | solution.py:178
  365.3 2.3 fusion.80
  368.7 3.9 copy.384
  372.6 4.7 reshape.433
  377.3 2.2 convolution_bitcast_fusion.2
  379.5 3.8 copy.387
  383.3 4.6 reshape.434
  387.9 2.2 constant_dynamic-update-slice_fusion.5
  391.4 2.4 copy-done
  394.5 2.3 collective-permute-start.3
  396.8 4.2 collective-permute-start.2
  403.3 2.5 reshape.436
  409.8 2.2 slice_bitcast_fusion.4
  413.9 61.9 %collective-permute-done.3 = bf16[32,4096]{1,0:T(8,128)(2,1)} collective-permute-done((bf16[32,4096]{1,0:T(8,128)(2,1)}, bf16[32,4096]{1,0:T(8,128)(2,1)}, u32[]{:S(2)}, u32[]{:S(2)}) %collective-permute-start.3) | collective-permute-done | bytes 262176 | tf_op jit(solution)/shard_map/ppermute | solution.py:22
  480.0 5.7 %scatter-add.9 = f32[4,32,4096]{2,0,1:T(4,128)S(1)} dynamic-update-slice(f32[4,32,4096]{2,0,1:T(4,128)S(1)} %copy.334, f32[1,32,4096]{2,0,1:T(1,128)S(1)} %copy_add_fusion, s32[]{:T(128)} %constant.155.clone.1, s32[]{:T(128)} %constant.154.clone.1, s32[]{:T(128)} %constant.154.clone.1) | dynamic-update-slice | bytes 1048580 | tf_op jit(solution)/shard_map/scatter-add | solution.py:188
  485.6 45.5 %all-reduce.6.cloned.1.call-done = f32[4,32,4096]{2,0,1:T(4,128)} async-done(((f32[4,32,4096]{2,0,1:T(4,128)}), f32[4,32,4096]{2,0,1:T(4,128)}) %all-reduce.6.cloned.1.call-update) | async-done | bytes 2097168 | tf_op jit(solution)/shard_map/psum | solution.py:199
  531.1 5.1 convolution_add_fusion.1
  536.2 7.7 %fusion = bf16[4,32,4096]{2,0,1:T(4,128)(2,1)S(1)} fusion(f32[4,32,4096]{2,0,1:T(4,128)} %convolution_add_fusion.1, bf16[16,32,4096]{2,1,0:T(8,128)(2,1)} %all-to-all-done.5, s32[16]{0:T(128)S(1)} %reduce_sum.48, pred[16]{0:T(512)(128)(4,1)S(1)} %reduce_or.18), kind=kOutput, calls=%fused_computation.6 | convolution fusion | flops 17825920 | bytes 7340112 | tf_op jit(solution)/shard_map/jr,rkc->jkc/dot_general | solution.py:210
  (145 shorter events, 51.0 us)
Async XLA Ops:
  7.2 16.4 %copy-start.23 = (bf16[64,4096]{1,0:T(8,128)(2,1)S(1)}, bf16[64,4096]{1,0:T(8,128)(2,1)}, u32[]{:S(2)}) copy-start(bf16[64,4096]{1,0:T(8,128)(2,1)} %param.13) | copy-start | bytes 1572868
  7.2 17.2 %copy-start.24 = (bf16[64,4096]{1,0:T(8,128)(2,1)S(1)}, bf16[64,4096]{1,0:T(8,128)(2,1)}, u32[]{:S(2)}) copy-start(bf16[64,4096]{1,0:T(8,128)(2,1)} %param.10) | copy-start | bytes 1572868
  9.2 10.9 %all-to-all-start.1 = ((bf16[64,2,2048]{2,0,1:T(8,128)(2,1)}), bf16[64,2,2048]{2,0,1:T(8,128)(2,1)S(1)}, u32[]{:S(2)}, u32[]{:S(2)}) async-start(bf16[64,2,2048]{2,0,1:T(8,128)(2,1)} %bitcast.255), calls=%async_computation.1 | async-start | bytes 1048576 | tf_op jit(solution)/shard_map/all_to_all | solution.py:36
  20.0 9.9 %all-to-all-start = ((bf16[64,2,2048]{2,0,1:T(8,128)(2,1)}), bf16[64,2,2048]{2,0,1:T(8,128)(2,1)S(1)}, u32[]{:S(2)}, u32[]{:S(2)}) async-start(bf16[64,2,2048]{2,0,1:T(8,128)(2,1)} %bitcast.256), calls=%async_computation | async-start | bytes 1048576 | tf_op jit(solution)/shard_map/all_to_all | solution.py:35
  30.0 8.9 %all-to-all-start.4 = ((bf16[64,2,2048]{2,0,1:T(8,128)(2,1)}), bf16[64,2,2048]{2,0,1:T(8,128)(2,1)S(1)}, u32[]{:S(2)}, u32[]{:S(2)}) async-start(bf16[64,2,2048]{2,0,1:T(8,128)(2,1)} %bitcast.253), calls=%async_computation.4 | async-start | bytes 1048576 | tf_op jit(solution)/shard_map/all_to_all | solution.py:37
  38.9 8.9 %all-to-all-start.3 = ((bf16[64,2,2048]{2,0,1:T(8,128)(2,1)}), bf16[64,2,2048]{2,0,1:T(8,128)(2,1)S(1)}, u32[]{:S(2)}, u32[]{:S(2)}) async-start(bf16[64,2,2048]{2,0,1:T(8,128)(2,1)} %bitcast.254), calls=%async_computation.3 | async-start | bytes 1048576 | tf_op jit(solution)/shard_map/all_to_all | solution.py:34
  47.0 11.5 %copy-start.25 = (s32[4]{0:T(128)S(1)}, s32[4]{0:T(128)}, u32[]{:S(2)}) copy-start(s32[4]{0:T(128)} %param.15) | copy-start | bytes 52
  47.8 198.7 %all-to-all-start.2 = ((bf16[16,32,4096]{2,1,0:T(8,128)(2,1)}), bf16[16,32,4096]{2,1,0:T(8,128)(2,1)}, u32[]{:S(2)}, u32[]{:S(2)}) async-start(bf16[16,32,4096]{2,1,0:T(8,128)(2,1)} %broadcast_select_fusion), calls=%async_computation.2 | async-start | bytes 8388608 | tf_op jit(solution)/shard_map/all_to_all | solution.py:80
  58.4 156.5 %all-reduce.8.cloned.1.call-start = ((), (), s32[]{:S(2)}) async-start(), calls=%async_computation.7 | async-start | bytes 2097152 | tf_op jit(solution)/shard_map/psum | solution.py:29
  71.0 88.1 %collective-permute-start = (bf16[32,4096]{1,0:T(8,128)(2,1)S(1)}, bf16[32,4096]{1,0:T(8,128)(2,1)S(1)}, u32[]{:S(2)}, u32[]{:S(2)}) collective-permute-start(bf16[32,4096]{1,0:T(8,128)(2,1)S(1)} %get-tuple-element.57), channel_id=1, source_target_pairs={{0,2},{2,4},{4,6},{6,8},{8,10},{10,12},{12,14},{14,16},{16,18},{18... | collective-permute-start | bytes 786440 | tf_op jit(solution)/shard_map/ppermute | solution.py:21
  74.4 86.8 %collective-permute-start.1 = (bf16[32,4096]{1,0:T(8,128)(2,1)S(1)}, bf16[32,4096]{1,0:T(8,128)(2,1)}, u32[]{:S(2)}, u32[]{:S(2)}) collective-permute-start(bf16[32,4096]{1,0:T(8,128)(2,1)S(1)} %get-tuple-element.58), channel_id=1, source_target_pairs={{2,0},{4,2},{6,4},{8,6},{10,8},{12,10},{14,12},{16,14},{18,16},{20... | collective-permute-start | bytes 786440 | tf_op jit(solution)/shard_map/ppermute | solution.py:22
  78.8 141.4 %copy-start.21 = (bf16[16,8,16,128]{3,2,1,0:T(8,128)(2,1)}, bf16[16,8,16,128]{3,2,1,0:T(8,128)(2,1)S(1)}, u32[]{:S(2)}) copy-start(bf16[16,8,16,128]{3,2,1,0:T(8,128)(2,1)S(1)} %copy.417) | copy-start | bytes 1572868
  220.5 0.8 copy-start.3
  229.6 4.7 copy-start.22
  234.5 24.0 %copy-start.11 = (bf16[4,32,16,128,1]{3,2,1,0,4:T(8,128)(2,1)}, bf16[4,32,16,128,1]{3,2,1,0,4:T(8,128)(2,1)S(1)}, u32[]{:S(2)}) copy-start(bf16[4,32,16,128,1]{3,2,1,0,4:T(8,128)(2,1)S(1)} %get-tuple-element.70) | copy-start | bytes 1572868
  251.2 2.4 copy-start.15
  251.2 2.5 copy-start.17
  258.5 3.6 copy-start.6
  270.2 3.3 copy-start.4
  270.2 3.3 copy-start.9
  298.1 3.3 copy-start.13
  298.1 3.3 copy-start.16
  304.8 6.9 %copy-start.7 = (bf16[4,6,4,16,8,128]{5,4,3,2,1,0:T(8,128)(2,1)S(1)}, bf16[4,6,4,16,8,128]{5,4,3,2,1,0:T(8,128)(2,1)}, u32[]{:S(2)}) copy-start(bf16[4,6,4,16,8,128]{5,4,3,2,1,0:T(8,128)(2,1)} %copy-done.6) | copy-start | bytes 9437188
  311.6 4.8 copy-start.2
  316.4 3.8 copy-start.1
  320.2 3.7 copy-start.20
  320.2 4.6 copy-start.12
  324.8 4.1 copy-start.5
  324.8 4.1 copy-start.14
  357.7 178.6 %all-to-all-start.5 = ((bf16[16,32,4096]{2,1,0:T(8,128)(2,1)}), bf16[16,32,4096]{2,1,0:T(8,128)(2,1)}, u32[]{:S(2)}, u32[]{:S(2)}) async-start(bf16[16,32,4096]{2,1,0:T(8,128)(2,1)} %scatter_fusion), calls=%async_computation.5 | async-start | bytes 8388608 | tf_op jit(solution)/shard_map/all_to_all | solution.py:178
  365.2 165.9 %all-reduce.6.cloned.1.call-start = ((), (), s32[]{:S(2)}) async-start(), calls=%async_computation.6 | async-start | bytes 4194304 | tf_op jit(solution)/shard_map/psum | solution.py:199
  365.3 3.4 copy-start.8
  387.9 2.8 copy-start.10
  390.9 2.9 copy-start
  390.9 10.1 %copy-start.19 = (bf16[4,16,32,4,32]{4,3,2,1,0:T(4,128)(2,1)S(1)}, bf16[4,16,32,4,32]{4,3,2,1,0:T(4,128)(2,1)}, u32[]{:S(2)}) copy-start(bf16[4,16,32,4,32]{4,3,2,1,0:T(4,128)(2,1)} %reshape.371) | copy-start | bytes 1572868
  394.5 81.3 %collective-permute-start.3 = (bf16[32,4096]{1,0:T(8,128)(2,1)}, bf16[32,4096]{1,0:T(8,128)(2,1)}, u32[]{:S(2)}, u32[]{:S(2)}) collective-permute-start(bf16[32,4096]{1,0:T(8,128)(2,1)} %get-tuple-element.44), channel_id=1, source_target_pairs={{2,0},{4,2},{6,4},{8,6},{10,8},{12,10},{14,12},{16,14},{18,16},{20... | collective-permute-start | bytes 786440 | tf_op jit(solution)/shard_map/ppermute | solution.py:22
  396.8 79.0 %collective-permute-start.2 = (bf16[32,4096]{1,0:T(8,128)(2,1)S(1)}, bf16[32,4096]{1,0:T(8,128)(2,1)}, u32[]{:S(2)}, u32[]{:S(2)}) collective-permute-start(bf16[32,4096]{1,0:T(8,128)(2,1)S(1)} %get-tuple-element.43), channel_id=1, source_target_pairs={{0,2},{2,4},{4,6},{6,8},{8,10},{10,12},{12,14},{14,16},{16,18},{18... | collective-permute-start | bytes 786440 | tf_op jit(solution)/shard_map/ppermute | solution.py:21
  406.6 1.2 copy-start.18
Sparse Core Ops, SparseCore 0:
  77.8 137.0 all-reduce.7
  409.9 121.1 all-reduce.5
where the time goes:
time: 562 us; the launch traced here: 554 us
  waiting for transfers between devices  252 us (45%)
  local copies, waits for them, and re-layouts  149 us (27%)
  matrix products  52.6 us (9%)
  starting transfers between devices  44.2 us (8%)
  other arithmetic  30.6 us (5%)
  between operations  25.2 us (4%)
    ppermute x2, waiting for transfers between devices, with_halo(): before = lax.ppermute(last, axis, up)  79.3 us
    ppermute x2, waiting for transfers between devices, with_halo(): after = lax.ppermute(first, axis, down)  63.9 us
    psum x1, waiting for transfers between devices, spread(): return lax.psum(jnp.where(mine, x, jnp.zeros_like(x)), axis)  51.6 us
    psum x1, waiting for transfers between devices, per_device(): far_sum = lax.psum(far_part, 'ctx')  45.5 us
    unnamed x64, local copies, waits for them, and re-layouts  17.3 us
  transfers between devices with their start and end apart: 12, of which 9 were waited for; matrix products, arithmetic and copies ran while one was open for 19% of the time, Pallas kernels for 0%

commit v1 on v0

v1 whole, which is shorter than its diff:
```python
import functools
import math

import jax
import jax.numpy as jnp
from jax import lax
from jax.experimental import pallas as pl
from jax.experimental.pallas import tpu as pltpu
from jax.sharding import PartitionSpec as P

DH = 128
BS = 32
NR = 3
NG = 4
F32 = jnp.float32
BF16 = jnp.bfloat16


def dot(a, b, dims):
    return lax.dot_general(a, b, (dims, ((), ())), preferred_element_type=F32)


def pick_kernel(idx_ref, x_ref, o_ref):
    o_ref[0] = x_ref[:, 0]


def pick(kv, idx):
    n, cols = idx.shape[0], kv.shape[3]
    return pl.pallas_call(
        pick_kernel,
        out_shape=jax.ShapeDtypeStruct((n, 2, BS, cols), BF16),
        grid_spec=pltpu.PrefetchScalarGridSpec(
            num_scalar_prefetch=1,
            grid=(n,),
            in_specs=[pl.BlockSpec((2, 1, BS, cols), lambda r, idx: (0, idx[r], 0, 0))],
            out_specs=pl.BlockSpec((1, 2, BS, cols), lambda r, idx: (r, 0, 0, 0)),
        ),
    )(idx, kv)


def attend_kernel(
    blocks, heads, sc, qg, kv, before, after, incoming, glob, dq, back, far, own, rim_a, rim_b
):
    inv_root = 1.0 / math.sqrt(DH)
    entries = blocks * NR
    for h in range(heads):
        c = slice(h * DH, (h + 1) * DH)
        back[:, :, :, c] = jnp.zeros((back.shape[0], 2, BS, DH), BF16)
        gk = [glob[i, 0, :, c] for i in range(NG)]
        gv = [glob[i, 1, :, c] for i in range(NG)]
        totals = [[None] * blocks, [None] * blocks]
        far_total = [None, None]

        def add(which, m, part):
            old = totals[which][m]
            totals[which][m] = part if old is None else old + part

        for n in range(blocks):
            rows = slice(n * BS, (n + 1) * BS)
            qn, gn = qg[0, rows, c], qg[1, rows, c]

            def listed(w, far_list):
                out = [
                    before[w, :, c] if n == 0 else kv[w, n - 1, :, c],
                    kv[w, n, :, c],
                    after[w, :, c] if n == blocks - 1 else kv[w, n + 1, :, c],
                ]
                out += [incoming[sc[n * NR + j], w, :, c] for j in range(NR)]
                return jnp.concatenate(out + far_list, axis=0)

            kn, vn = listed(0, gk), listed(1, gv)
            s = dot(qn, kn, ((1,), (1,))) * inv_root
            dp = dot(gn, vn, ((1,), (1,)))
            if n == 0 or n == blocks - 1:
                col = lax.broadcasted_iota(jnp.int32, s.shape, 1)
                if n == 0:
                    s = jnp.where(col < sc[entries], -jnp.inf, s)
                if n == blocks - 1:
                    bad = (col >= 2 * BS) & (col < 2 * BS + sc[entries + 1])
                    s = jnp.where(bad, -jnp.inf, s)
            e = jnp.exp(s - jnp.max(s, axis=1, keepdims=True))
            p = e / jnp.sum(e, axis=1, keepdims=True)
            ph = p.astype(BF16)
            row_dot = jnp.sum(ph.astype(F32) * dp, axis=1, keepdims=True)
            ds = (p * (dp - row_dot)).astype(BF16)
            dq[rows, c] = (dot(ds, kn, ((1,), (0,))) * inv_root).astype(BF16)
            for w, part in (
                (0, dot(ds, qn, ((0,), (0,))) * inv_root),
                (1, dot(ph, gn, ((0,), (0,)))),
            ):
                if n == 0:
                    rim_a[w, :, c] = part[:BS].astype(BF16)
                else:
                    add(w, n - 1, part[:BS])
                add(w, n, part[BS : 2 * BS])
                if n == blocks - 1:
                    rim_b[w, :, c] = part[2 * BS : 3 * BS].astype(BF16)
                else:
                    add(w, n + 1, part[2 * BS : 3 * BS])
                for j in range(NR):
                    piece = part[(3 + j) * BS : (4 + j) * BS].astype(BF16)
                    back[sc[n * NR + j], w, :, c] = piece
                tail = part[(3 + NR) * BS :]
                far_total[w] = tail if far_total[w] is None else far_total[w] + tail
        for w in range(2):
            for m in range(blocks):
                own[w, m, :, c] = totals[w][m]
            for i in range(NG):
                far[i, w, :, c] = far_total[w][i * BS : (i + 1) * BS].astype(BF16)


def finish_kernel(blocks, devices, sc, own, arrived, far, rim_a, rim_b, dk, dv, acc):
    acc[...] = own[...]
    acc[:, 0] += rim_a[...].astype(F32)
    acc[:, blocks - 1] += rim_b[...].astype(F32)
    for r in range(devices):
        @pl.when(sc[r] < blocks)
        def _():
            acc[:, sc[r]] += arrived[r].astype(F32)
    for g in range(NG):
        @pl.when(sc[devices + g] < blocks)
        def _():
            acc[:, sc[devices + g]] += far[g].astype(F32)
    for w, out in ((0, dk), (1, dv)):
        for m in range(blocks):
            out[m * BS : (m + 1) * BS, :] = acc[w, m].astype(BF16)


def columns(shape, cols):
    lead = (0,) * (len(shape) - 1)
    return pl.BlockSpec(tuple(shape[:-1]) + (cols,), lambda i, *_: lead + (i,))


def by_columns(kernel, scalars, arrays, outs, cols, scratch=()):
    steps = arrays[0].shape[-1] // cols
    return pl.pallas_call(
        kernel,
        out_shape=outs,
        grid_spec=pltpu.PrefetchScalarGridSpec(
            num_scalar_prefetch=1,
            grid=(steps,),
            in_specs=[columns(a.shape, cols) for a in arrays],
            out_specs=[columns(o.shape, cols) for o in outs],
            scratch_shapes=scratch,
        ),
        compiler_params=pltpu.CompilerParams(vmem_limit_bytes=40 * 2**20),
    )(scalars, *arrays)


def to_heads(x, y):
    return lax.all_to_all(jnp.stack([x, y]), "head", split_axis=2, concat_axis=1, tiled=True)


def exchange(x):
    return lax.all_to_all(x, "ctx", split_axis=0, concat_axis=0, tiled=True)


def per_device(queries, key_states, value_states, out_grad, random_blocks, global_blocks):
    kv = to_heads(key_states, value_states)
    qg = to_heads(queries, out_grad)
    tokens, cols = kv.shape[1:]
    blocks = tokens // BS
    devices = lax.axis_size("ctx")
    me = lax.axis_index("ctx")
    entries = blocks * NR
    up = [(i, i + 1) for i in range(devices - 1)]
    down = [(j, i) for i, j in up]
    kv = kv.reshape(2, blocks, BS, cols)

    table = random_blocks.reshape(devices, entries)
    served = table // blocks == me
    served_block = jnp.sum(jnp.where(served, table % blocks, 0), axis=1)
    served_used = jnp.any(served, axis=1)
    my_owner = lax.dynamic_index_in_dim(table, me, 0, keepdims=False) // blocks
    global_owner = global_blocks // blocks
    global_offset = global_blocks % blocks
    edge = jnp.stack([jnp.where(me == 0, BS, 0), jnp.where(me == devices - 1, BS, 0)])
    attend_scalars = jnp.concatenate([my_owner, edge]).astype(jnp.int32)
    finish_scalars = jnp.concatenate(
        [
            jnp.where(served_used, served_block, blocks),
            jnp.where(global_owner == me, global_offset, blocks),
        ]
    ).astype(jnp.int32)

    rows = NG * 2 * BS // devices
    pieces = exchange(pick(kv, global_offset).reshape(devices, rows, cols))
    source = jnp.take(global_owner, me * NG // devices)
    piece = lax.dynamic_index_in_dim(pieces, source, 0, keepdims=True)
    glob = exchange(jnp.broadcast_to(piece, (devices, rows, cols))).reshape(NG, 2, BS, cols)
    incoming = exchange(pick(kv, served_block))
    before = lax.ppermute(kv[:, blocks - 1], "ctx", up)
    after = lax.ppermute(kv[:, 0], "ctx", down)

    width = 2 * DH if cols % (2 * DH) == 0 else DH
    shape = jax.ShapeDtypeStruct
    dq, back, far, own, rim_a, rim_b = by_columns(
        functools.partial(attend_kernel, blocks, width // DH),
        attend_scalars,
        [qg, kv, before, after, incoming, glob],
        [
            shape((tokens, cols), BF16),
            shape((devices, 2, BS, cols), BF16),
            shape((NG, 2, BS, cols), BF16),
            shape((2, blocks, BS, cols), F32),
            shape((2, BS, cols), BF16),
            shape((2, BS, cols), BF16),
        ],
        width,
    )

    far_parts = exchange(far.reshape(devices, rows, cols))
    far_piece = jnp.sum(far_parts.astype(F32), axis=0, keepdims=True).astype(BF16)
    arrived = exchange(back)
    far_sum = exchange(jnp.broadcast_to(far_piece, (devices, rows, cols))).reshape(NG, 2, BS, cols)
    from_next = lax.ppermute(rim_a, "ctx", down)
    from_last = lax.ppermute(rim_b, "ctx", up)
    dk, dv = by_columns(
        functools.partial(finish_kernel, blocks, devices),
        finish_scalars,
        [own, arrived, far_sum, from_last, from_next],
        [shape((tokens, cols), BF16)] * 2,
        width,
        [pltpu.VMEM((2, blocks, BS, width), F32)],
    )
    return dq, dk, dv


def solution(mesh):
    placed = P(("ctx", "head"), None)
    return jax.shard_map(
        per_device,
        mesh=mesh,
        in_specs=(placed, placed, placed, placed, P(), P()),
        out_specs=(P("ctx", "head"), P("ctx", "head"), P("ctx", "head")),
        check_vma=False,
    )
```

time: 562 us -> 424 us (0.75); the launches traced: 554 us -> 423 us
  local copies, waits for them, and re-layouts: 149 us -> 32.8 us
  blocking collectives: 0 us -> 58.8 us
  Pallas kernels: 0 us -> 57.2 us
  matrix products: 52.6 us -> 0 us
  other arithmetic: 30.6 us -> 3.07 us
  waiting for transfers between devices: 252 us -> 227 us
  between operations: 25.2 us -> 1.51 us
    psum x2 -> x0, waiting for transfers between devices: 97.1 us -> none  [the longest x1 51.6 us: spread(): return lax.psum(jnp.where(mine, x, jnp.zeros_like(x)), axis)]
    all_to_all x0 -> x2, blocking collectives: none -> 58.8 us  [exchange(): return lax.all_to_all(x, 'ctx', split_axis=0, concat_axis=0, tiled=True)]
    reshape x20 -> x1, local copies, waits for them, and re-layouts: 58.4 us -> 0.07 us  [per_device(): table = random_blocks.reshape(devices, entries)]
    pallas_call x0 -> x4, Pallas kernels: none -> 57.2 us  [the longest x2 42.5 us: by_columns(): pl.pallas_call(kernel, out_shape=outs, grid_spec=pltpu.PrefetchScalarGrid...]
    dot_general x16 -> x0, matrix products: 52.6 us -> none  [the longest x1 7.73 us: per_device(): jnp.einsum('jr,rkc->jkc', weights, arrived, preferred_element_type=jnp.fl...]
    all_to_all x6, waiting for transfers between devices: 11.5 us -> 57 us  [the longest x4 33.1 us: exchange(): return lax.all_to_all(x, 'ctx', split_axis=0, concat_axis=0, tiled=True)]
    ppermute x4, waiting for transfers between devices: 143 us -> 170 us  [the longest x1 88 us: per_device(): from_last = lax.ppermute(rim_b, 'ctx', up)]
    slice x11 -> x0, local copies, waits for them, and re-layouts: 15.7 us -> none  [the longest x2 7.5 us: per_device(): random_part = key_value_parts(near_ds[:, :, :, 3:], near_probs[:, :, :, 3:])]
  transfers between devices with their start and end apart: 12 -> 10, of which waited for: 9 -> 7; matrix products, arithmetic and copies ran while one was open for 19% -> 4% of each run, Pallas kernels for 0% -> 2%
where the time goes in v1:
time: 424 us; the launch traced here: 423 us
  waiting for transfers between devices  227 us (54%)
  blocking collectives  58.8 us (14%)
  Pallas kernels  57.2 us (13%)
  starting transfers between devices  42.1 us (10%)
  local copies, waits for them, and re-layouts  32.8 us (8%)
    ppermute x1, waiting for transfers between devices, per_device(): from_last = lax.ppermute(rim_b, 'ctx', up)  88 us
    ppermute x1, waiting for transfers between devices, per_device(): after = lax.ppermute(kv[:, 0], 'ctx', down)  80.7 us
    all_to_all x2, blocking collectives, exchange(): return lax.all_to_all(x, 'ctx', split_axis=0, concat_axis=0, tiled=True)  58.8 us
    pallas_call x2, Pallas kernels, by_columns(): pl.pallas_call(kernel, out_shape=outs, grid_spec=pltpu.PrefetchScalarGrid...  42.5 us
    all_to_all x4, waiting for transfers between devices, exchange(): return lax.all_to_all(x, 'ctx', split_axis=0, concat_axis=0, tiled=True)  33.1 us
    all_to_all x2, waiting for transfers between devices, to_heads(): lax.all_to_all(jnp.stack([x, y]), 'head', split_axis=2, concat_axis=1, ti...  23.8 us
    all_to_all x4, starting transfers between devices, exchange(): return lax.all_to_all(x, 'ctx', split_axis=0, concat_axis=0, tiled=True)  23.2 us
    unnamed x31, local copies, waits for them, and re-layouts  15.1 us
  transfers between devices with their start and end apart: 10, of which 7 were waited for; matrix products, arithmetic and copies ran while one was open for 4% of the time, Pallas kernels for 2%

profile of v1, /device:TPU:13, one launch (start us, length us, event | category | flops | bytes accessed | tf_op | source)
XLA Modules:
  0.0 422.6 jit_solution(18027197977541640211)
XLA Ops:
  0.6 1.3 pad_maximum_fusion.1
  1.9 2.8 copy.35
  4.8 0.0 copy-start.12
  4.8 2.4 reshape.69
  7.2 3.6 all-to-all-start.1
  10.8 0.0 copy-done.12
  10.8 0.5 compare_select_fusion
  11.4 12.4 %all-to-all-done.1 = bf16[2,2,131072]{2,1,0:T(2,128)(2,1)S(1)} async-done(((bf16[2,2,131072]{2,1,0:T(2,128)(2,1)}), bf16[2,2,131072]{2,1,0:T(2,128)(2,1)S(1)}, u32[]{:S(2)}, u32[]{:S(2)}) %all-to-all-start.1) | async-done | bytes 1048608 | tf_op jit(solution)/shard_map/all_to_all | solution.py:151
  23.8 1.3 reshape.70
  25.1 3.6 copy.37
  28.8 4.2 shard_map.86
  32.9 7.4 %all-to-all-start.3 = ((bf16[16,16,2048]{2,1,0:T(8,128)(2,1)}), bf16[16,16,2048]{2,1,0:T(8,128)(2,1)}, u32[]{:S(2)}, u32[]{:S(2)}) async-start(bf16[16,16,2048]{2,1,0:T(8,128)(2,1)} %bitcast.55), calls=%async_computation.3 | async-start | bytes 2097152 | tf_op jit(solution)/shard_map/all_to_all | solution.py:155
  40.4 0.0 copy-done.8
  40.4 0.0 copy-done.9
  40.4 0.1 pad_maximum_fusion
  40.5 2.8 copy.33
  43.3 2.5 reshape.67
  45.8 19.5 %all-to-all-done.3 = bf16[16,16,2048]{2,1,0:T(8,128)(2,1)} async-done(((bf16[16,16,2048]{2,1,0:T(8,128)(2,1)}), bf16[16,16,2048]{2,1,0:T(8,128)(2,1)}, u32[]{:S(2)}, u32[]{:S(2)}) %all-to-all-start.3) | async-done | bytes 1048608 | tf_op jit(solution)/shard_map/all_to_all | solution.py:155
  65.3 3.6 all-to-all-start
  68.9 0.0 copy-start.10
  69.0 0.6 dynamic-slice.2
  70.2 0.8 dynamic-slice_bitcast_fusion
  71.1 11.4 %all-to-all-done = bf16[2,2,131072]{2,1,0:T(2,128)(2,1)S(1)} async-done(((bf16[2,2,131072]{2,1,0:T(2,128)(2,1)}), bf16[2,2,131072]{2,1,0:T(2,128)(2,1)S(1)}, u32[]{:S(2)}, u32[]{:S(2)}) %all-to-all-start) | async-done | bytes 1048608 | tf_op jit(solution)/shard_map/all_to_all | solution.py:151
  82.4 1.1 broadcast_in_dim.27
  83.5 5.7 %all-to-all-start.4 = ((bf16[16,16,2048]{2,1,0:T(8,128)(2,1)}), bf16[16,16,2048]{2,1,0:T(8,128)(2,1)S(1)}, u32[]{:S(2)}, u32[]{:S(2)}) async-start(bf16[16,16,2048]{2,1,0:T(8,128)(2,1)} %broadcast_in_dim.27), calls=%async_computation.4 | async-start | bytes 2097152 | tf_op jit(solution)/shard_map/all_to_all | solution.py:155
  89.3 0.0 copy-done.10
  89.3 0.1 reduce_sum.29
  89.4 0.7 reduce_sum.30.idx_ref
  90.1 10.5 %shard_map.85 = bf16[16,2,32,2048]{3,2,1,0:T(8,128)(2,1)} custom-call(s32[16]{0:T(128)} %reduce_sum.30.idx_ref, bf16[2,4,32,2048]{3,2,1,0:T(8,128)(2,1)} %bitcast.44), custom_call_target="tpu_custom_call" | custom-call | tf_op jit(solution)/shard_map/pallas_call | solution.py:29
  100.5 13.6 %all-to-all-done.4 = bf16[16,16,2048]{2,1,0:T(8,128)(2,1)S(1)} async-done(((bf16[16,16,2048]{2,1,0:T(8,128)(2,1)}), bf16[16,16,2048]{2,1,0:T(8,128)(2,1)S(1)}, u32[]{:S(2)}, u32[]{:S(2)}) %all-to-all-start.4) | async-done | bytes 1048608 | tf_op jit(solution)/shard_map/all_to_all | solution.py:155
  114.1 4.9 %all-to-all-start.2 = ((bf16[16,2,32,2048]{3,2,1,0:T(8,128)(2,1)}), bf16[16,2,32,2048]{3,2,1,0:T(8,128)(2,1)}, u32[]{:S(2)}, u32[]{:S(2)}) async-start(bf16[16,2,32,2048]{3,2,1,0:T(8,128)(2,1)} %shard_map.85), calls=%async_computation.2 | async-start | bytes 8388608 | tf_op jit(solution)/shard_map/all_to_all | solution.py:155
  119.1 0.0 copy-done
  119.1 0.8 slice_bitcast_fusion
  119.9 2.3 collective-permute-start.1
  122.2 4.2 collective-permute-start
  126.4 0.1 copy.32
  126.5 0.1 reshape.32
  126.6 0.1 pad_add_fusion.sc
  126.7 2.3 reshape.68
  129.0 4.6 %copy.34 = bf16[2,64,2,2048]{3,1,2,0:T(8,128)(2,1)S(1)} copy(bf16[2,64,2,2048]{1,0,3,2:T(2,128)(2,1)} %bitcast.54) | data formatting | bytes 2097152 | tf_op jit(solution)/shard_map/all_to_all | solution.py:151
  133.6 80.7 %collective-permute-done.1.after = bf16[2,32,2048]{2,1,0:T(8,128)(2,1)S(1)} collective-permute-done((bf16[2,32,2048]{2,1,0:T(8,128)(2,1)}, bf16[2,32,2048]{2,1,0:T(8,128)(2,1)S(1)}, u32[]{:S(2)}, u32[]{:S(2)}) %collective-permute-start.1) | collective-permute-done | bytes 262176 | tf_op jit(solution)/shard_map/ppermute | solution.py:193
  214.3 0.0 collective-permute-done.before
  214.3 0.0 all-to-all-done.2.incoming
  214.3 35.2 %shard_map.87 = (bf16[128,2048]{1,0:T(8,128)(2,1)}, bf16[16,2,32,2048]{3,2,1,0:T(8,128)(2,1)S(1)}, bf16[4,2,32,2048]{3,2,1,0:T(8,128)(2,1)S(1)}, f32[2,4,32,2048...) custom-call(s32[14]{0:T(128)S(1)} %pad_add_fusion.sc, ...), custom_call_target="tpu_custom_call" | custom-call | tf_op jit(solution)/shard_map/pallas_call | solution.py:136
  249.4 2.0 copy-done.1
  251.4 1.4 copy-done.2
  252.8 0.7 copy-done.6
  253.5 0.7 copy-done.7
  254.2 29.2 %all_to_all.63 = bf16[16,16,2048]{2,1,0:T(8,128)(2,1)S(1)} all-to-all(bf16[16,16,2048]{2,1,0:T(8,128)(2,1)S(1)} %bitcast.50), channel_id=1, replica_groups=mesh['ctx'=16,'head'=2] {'ctx'}, dimensions={0} | all-to-all | bytes 2097152 | tf_op jit(solution)/shard_map/all_to_all | solution.py:155
  283.4 0.1 reduce_sum.31
  283.5 0.1 broadcast_in_dim.29
  283.7 29.6 %all_to_all.64 = bf16[16,16,2048]{2,1,0:T(8,128)(2,1)S(1)} all-to-all(bf16[16,16,2048]{2,1,0:T(8,128)(2,1)S(1)} %broadcast_in_dim.29), channel_id=1, replica_groups=mesh['ctx'=16,'head'=2] {'ctx'}, dimensions={0} | all-to-all | bytes 2097152 | tf_op jit(solution)/shard_map/all_to_all | solution.py:155
  313.3 5.1 %all-to-all-start.5 = ((bf16[16,2,32,2048]{3,2,1,0:T(8,128)(2,1)}), bf16[16,2,32,2048]{3,2,1,0:T(8,128)(2,1)}, u32[]{:S(2)}, u32[]{:S(2)}) async-start(bf16[16,2,32,2048]{3,2,1,0:T(8,128)(2,1)} %copy-done.1), calls=%async_computation.5 | async-start | bytes 8388608 | tf_op jit(solution)/shard_map/all_to_all | solution.py:155
  318.4 0.1 reduce_or.14
  318.5 0.1 reduce_or.18
  318.6 3.3 collective-permute-start.2
  322.0 1.9 collective-permute-start.3
  323.9 0.1 pad_add_fusion.1.sc
  324.0 88.0 %collective-permute-done.2.rim_a = bf16[2,32,2048]{2,1,0:T(8,128)(2,1)S(1)} collective-permute-done((bf16[2,32,2048]{2,1,0:T(8,128)(2,1)}, bf16[2,32,2048]{2,1,0:T(8,128)(2,1)S(1)}, u32[]{:S(2)}, u32[]{:S(2)}) %collective-permute-start.2) | collective-permute-done | bytes 262176 | tf_op jit(solution)/shard_map/ppermute | solution.py:217
  412.0 1.6 collective-permute-done.3.rim_b
  413.6 0.7 copy-done.4
  414.3 0.0 all-to-all-done.5.arrived
  414.3 0.9 copy-done.5
  415.3 7.4 %shard_map.88 = (bf16[128,2048]{1,0:T(8,128)(2,1)}, bf16[128,2048]{1,0:T(8,128)(2,1)}) custom-call(s32[20]{0:T(128)S(1)} %pad_add_fusion.1.sc, f32[2,4,32,2048]{3,2,1,0:T(8,128)S(1)} %copy-done.3, bf16[16,2,32,2048]{3,2,1,0:T(8,128)(2,1)} %all-to-all-done.5.arrived, bf16[4,2,32,2048]{3,2,1,0:T(8,128)(2,1)S(1)} %bitcast.49, ...), custom_call_target="tpu_custom_call" | custom-call | tf_op jit(solution)/shard_map/pallas_call | solution.py:136
  (17 shorter events, 0.1 us)
Async XLA Ops:
  4.8 6.0 %copy-start.12 = (s32[4]{0:T(128)S(1)}, s32[4]{0:T(128)}, u32[]{:S(2)}) copy-start(s32[4]{0:T(128)} %param.11) | copy-start | bytes 52
  7.2 16.6 %all-to-all-start.1 = ((bf16[2,2,131072]{2,1,0:T(2,128)(2,1)}), bf16[2,2,131072]{2,1,0:T(2,128)(2,1)S(1)}, u32[]{:S(2)}, u32[]{:S(2)}) async-start(bf16[2,2,131072]{2,1,0:T(2,128)(2,1)} %reshape.69), calls=%async_computation.1 | async-start | bytes 2097152 | tf_op jit(solution)/shard_map/all_to_all | solution.py:151
  28.8 11.6 %copy-start.8 = (bf16[64,4096]{1,0:T(8,128)(2,1)S(1)}, bf16[64,4096]{1,0:T(8,128)(2,1)}, u32[]{:S(2)}) copy-start(bf16[64,4096]{1,0:T(8,128)(2,1)} %param.9) | copy-start | bytes 1572868
  28.8 11.6 %copy-start.9 = (bf16[64,4096]{1,0:T(8,128)(2,1)S(1)}, bf16[64,4096]{1,0:T(8,128)(2,1)}, u32[]{:S(2)}) copy-start(bf16[64,4096]{1,0:T(8,128)(2,1)} %param.6) | copy-start | bytes 1572868
  32.9 32.4 %all-to-all-start.3 = ((bf16[16,16,2048]{2,1,0:T(8,128)(2,1)}), bf16[16,16,2048]{2,1,0:T(8,128)(2,1)}, u32[]{:S(2)}, u32[]{:S(2)}) async-start(bf16[16,16,2048]{2,1,0:T(8,128)(2,1)} %bitcast.55), calls=%async_computation.3 | async-start | bytes 2097152 | tf_op jit(solution)/shard_map/all_to_all | solution.py:155
  65.3 17.1 %all-to-all-start = ((bf16[2,2,131072]{2,1,0:T(2,128)(2,1)}), bf16[2,2,131072]{2,1,0:T(2,128)(2,1)S(1)}, u32[]{:S(2)}, u32[]{:S(2)}) async-start(bf16[2,2,131072]{2,1,0:T(2,128)(2,1)} %reshape.67), calls=%async_computation | async-start | bytes 2097152 | tf_op jit(solution)/shard_map/all_to_all | solution.py:151
  68.9 20.3 %copy-start.10 = (s32[64,3]{0,1:T(4,128)S(1)}, s32[64,3]{0,1:T(4,128)}, u32[]{:S(2)}) copy-start(s32[64,3]{0,1:T(4,128)} %param.10) | copy-start | bytes 2308
  83.5 30.6 %all-to-all-start.4 = ((bf16[16,16,2048]{2,1,0:T(8,128)(2,1)}), bf16[16,16,2048]{2,1,0:T(8,128)(2,1)S(1)}, u32[]{:S(2)}, u32[]{:S(2)}) async-start(bf16[16,16,2048]{2,1,0:T(8,128)(2,1)} %broadcast_in_dim.27), calls=%async_computation.4 | async-start | bytes 2097152 | tf_op jit(solution)/shard_map/all_to_all | solution.py:155
  100.5 18.5 %copy-start = (bf16[2,2,64,2048]{3,2,1,0:T(8,128)(2,1)S(1)}, bf16[2,2,64,2048]{3,2,1,0:T(8,128)(2,1)}, u32[]{:S(2)}) copy-start(bf16[2,2,64,2048]{3,2,1,0:T(8,128)(2,1)} %copy.37) | copy-start | bytes 3145732
  114.1 100.1 %all-to-all-start.2 = ((bf16[16,2,32,2048]{3,2,1,0:T(8,128)(2,1)}), bf16[16,2,32,2048]{3,2,1,0:T(8,128)(2,1)}, u32[]{:S(2)}, u32[]{:S(2)}) async-start(bf16[16,2,32,2048]{3,2,1,0:T(8,128)(2,1)} %shard_map.85), calls=%async_computation.2 | async-start | bytes 8388608 | tf_op jit(solution)/shard_map/all_to_all | solution.py:155
  119.9 94.3 %collective-permute-start.1 = (bf16[2,32,2048]{2,1,0:T(8,128)(2,1)}, bf16[2,32,2048]{2,1,0:T(8,128)(2,1)S(1)}, u32[]{:S(2)}, u32[]{:S(2)}) collective-permute-start(bf16[2,32,2048]{2,1,0:T(8,128)(2,1)} %get-tuple-element.35), channel_id=1, source_target_pairs={{2,0},{4,2},{6,4},{8,6},{10,8},{12,10},{14,12},{16,14},{18,16},{20... | collective-permute-start | bytes 786440 | tf_op jit(solution)/shard_map/ppermute | solution.py:193
  122.2 92.1 %collective-permute-start = (bf16[2,32,2048]{2,1,0:T(8,128)(2,1)}, bf16[2,32,2048]{2,1,0:T(8,128)(2,1)}, u32[]{:S(2)}, u32[]{:S(2)}) collective-permute-start(bf16[2,32,2048]{2,1,0:T(8,128)(2,1)} %get-tuple-element.36), channel_id=1, source_target_pairs={{0,2},{2,4},{4,6},{6,8},{8,10},{10,12},{12,14},{14,16},{16,18},{18... | collective-permute-start | bytes 786440 | tf_op jit(solution)/shard_map/ppermute | solution.py:192
  249.4 2.0 copy-start.1
  251.4 1.4 copy-start.2
  252.8 0.7 copy-start.6
  253.5 0.7 copy-start.7
  313.3 10.6 %copy-start.11 = (s32[16]{0:T(128)S(1)}, s32[16]{0:T(128)}, u32[]{:S(2)}) copy-start(s32[16]{0:T(128)} %reduce_sum.30.idx_ref) | copy-start | bytes 196
  313.3 101.0 %copy-start.3 = (f32[2,4,32,2048]{3,2,1,0:T(8,128)S(1)}, f32[2,4,32,2048]{3,2,1,0:T(8,128)}, u32[]{:S(2)}) copy-start(f32[2,4,32,2048]{3,2,1,0:T(8,128)} %copy-done.2) | copy-start | bytes 6291460
  313.3 101.0 %all-to-all-start.5 = ((bf16[16,2,32,2048]{3,2,1,0:T(8,128)(2,1)}), bf16[16,2,32,2048]{3,2,1,0:T(8,128)(2,1)}, u32[]{:S(2)}, u32[]{:S(2)}) async-start(bf16[16,2,32,2048]{3,2,1,0:T(8,128)(2,1)} %copy-done.1), calls=%async_computation.5 | async-start | bytes 8388608 | tf_op jit(solution)/shard_map/all_to_all | solution.py:155
  318.6 93.3 %collective-permute-start.2 = (bf16[2,32,2048]{2,1,0:T(8,128)(2,1)}, bf16[2,32,2048]{2,1,0:T(8,128)(2,1)S(1)}, u32[]{:S(2)}, u32[]{:S(2)}) collective-permute-start(bf16[2,32,2048]{2,1,0:T(8,128)(2,1)} %copy-done.7), channel_id=1, source_target_pairs={{0,2},{2,4},{4,6},{6,8},{8,10},{10,12},{12,14},{14,16},{16,18},{18... | collective-permute-start | bytes 786440 | tf_op jit(solution)/shard_map/ppermute | solution.py:217
  322.0 91.6 %collective-permute-start.3 = (bf16[2,32,2048]{2,1,0:T(8,128)(2,1)}, bf16[2,32,2048]{2,1,0:T(8,128)(2,1)S(1)}, u32[]{:S(2)}, u32[]{:S(2)}) collective-permute-start(bf16[2,32,2048]{2,1,0:T(8,128)(2,1)} %copy-done.6), channel_id=1, source_target_pairs={{2,0},{4,2},{6,4},{8,6},{10,8},{12,10},{14,12},{16,14},{18,16},{20... | collective-permute-start | bytes 786440 | tf_op jit(solution)/shard_map/ppermute | solution.py:216
  413.6 0.7 copy-start.4
  414.3 1.0 copy-start.5

commit v2 on v1

--- a/solution.py
+++ b/solution.py
@@ -147,24 +147,211 @@
     )(scalars, *arrays)
 
 
+MESH = pl.DeviceIdType.MESH
+ANY = pl.BlockSpec(memory_space=pl.ANY)
+VMEM = pl.BlockSpec(memory_space=pltpu.VMEM)
+SMEM = pl.BlockSpec(memory_space=pltpu.SMEM)
+
+
+def others(axis, n, body, first=1, last=None):
+    me = lax.axis_index(axis)
+
+    def step(d, carry):
+        body(lax.rem(me + d, n))
+        return carry
+
+    lax.fori_loop(first, n if last is None else last, step, 0)
+
+
+def meet(axes):
+    barrier = pltpu.get_barrier_semaphore()
+    for axis, n in axes:
+        others(axis, n, lambda p: pl.semaphore_signal(
+            barrier, inc=1, device_id={axis: p}, device_id_type=MESH))
+    pl.semaphore_wait(barrier, sum(n - 1 for _, n in axes))
+
+
+def head_exchange(n, xs, out, send, recv, local):
+    me = lax.axis_index("head")
+    rows, cols = xs[0].shape[0], out.shape[2]
+
+    def copy(i, p):
+        return pltpu.make_async_remote_copy(
+            src_ref=xs[i].at[:, pl.ds(pl.multiple_of(p * cols, DH), cols)],
+            dst_ref=out.at[i, pl.ds(pl.multiple_of(me * rows, rows), rows)],
+            send_sem=send.at[i, p],
+            recv_sem=recv.at[i, me],
+            device_id={"head": p},
+            device_id_type=MESH,
+        )
+
+    def arrival(i, p):
+        return pltpu.make_async_remote_copy(
+            src_ref=xs[i].at[:, pl.ds(pl.multiple_of(p * cols, DH), cols)],
+            dst_ref=out.at[i, pl.ds(pl.multiple_of(p * rows, rows), rows)],
+            send_sem=send.at[i, p],
+            recv_sem=recv.at[i, p],
+            device_id={"head": p},
+            device_id_type=MESH,
+        )
+
+    def own(i):
+        return pltpu.make_async_copy(
+            xs[i].at[:, pl.ds(pl.multiple_of(me * cols, DH), cols)],
+            out.at[i, pl.ds(pl.multiple_of(me * rows, rows), rows)],
+            local.at[i],
+        )
+
+    for i in range(2):
+        others("head", n, lambda p: copy(i, p).start())
+        own(i).start()
+
+    def wait():
+        for i in range(2):
+            others("head", n, lambda p: arrival(i, p).wait())
+            own(i).wait()
+
+    return wait
+
+
+def heads_kernel(n, x, y, out, send, recv, local):
+    meet([("head", n)])
+    head_exchange(n, (x, y), out, send, recv, local)()
+
+
+def head_sems(n):
+    return [
+        pltpu.SemaphoreType.DMA((2, n)),
+        pltpu.SemaphoreType.DMA((2, n)),
+        pltpu.SemaphoreType.DMA((2,)),
+    ]
+
+
 def to_heads(x, y):
-    return lax.all_to_all(jnp.stack([x, y]), "head", split_axis=2, concat_axis=1, tiled=True)
-
-
-def exchange(x):
-    return lax.all_to_all(x, "ctx", split_axis=0, concat_axis=0, tiled=True)
+    n = lax.axis_size("head")
+    rows, cols = x.shape
+    return pl.pallas_call(
+        functools.partial(heads_kernel, n),
+        out_shape=jax.ShapeDtypeStruct((2, rows * n, cols // n), BF16),
+        in_specs=[ANY, ANY],
+        out_specs=ANY,
+        scratch_shapes=head_sems(n),
+        compiler_params=pltpu.CompilerParams(collective_id=0, has_side_effects=True),
+    )(x, y)
+
+
+def all_to_all(n, src, dst, send, recv, local):
+    me = lax.axis_index("ctx")
+
+    def copy(slot, p):
+        return pltpu.make_async_remote_copy(
+            src_ref=src(p),
+            dst_ref=dst.at[slot],
+            send_sem=send.at[p],
+            recv_sem=recv.at[slot],
+            device_id={"ctx": p},
+            device_id_type=MESH,
+        )
+
+    own = pltpu.make_async_copy(src(me), dst.at[me], local)
+
+    def start(first=1, last=None):
+        others("ctx", n, lambda p: copy(me, p).start(), first, last)
+        if first == 1:
+            own.start()
+
+    def wait():
+        others("ctx", n, lambda p: copy(p, p).wait())
+        own.wait()
+
+    return start, wait
+
+
+def trade_kernel(n, hn, source, parts, blocks, to_next, to_last, *refs):
+    forward = hn > 0
+    if forward:
+        q, g, parts_out, blocks_out, from_last, from_next, qg = refs[:7]
+        refs = refs[7:]
+    else:
+        parts_out, blocks_out, from_last, from_next = refs[:4]
+        refs = refs[4:]
+    got, piece, s1, r1, s2, r2, s3, r3, s4, r4, local = refs[:11]
+    me = lax.axis_index("ctx")
+    after, before = lax.rem(me + 1, n), lax.rem(me + n - 1, n)
+    meet([("ctx", n)] + ([("head", hn)] if forward else []))
+    start1, wait1 = all_to_all(n, lambda p: parts.at[p], got, s1, r1, local.at[0])
+    start2, wait2 = all_to_all(n, lambda p: piece, parts_out, s2, r2, local.at[1])
+    start3, wait3 = all_to_all(n, lambda p: blocks.at[p], blocks_out, s3, r3, local.at[2])
+    start1()
+    if forward:
+        wait_heads = head_exchange(hn, (q, g), qg, *refs[11:])
+    edges = [
+        pltpu.make_async_remote_copy(
+            src_ref=a,
+            dst_ref=b,
+            send_sem=s4.at[i],
+            recv_sem=r4.at[i],
+            device_id={"ctx": p},
+            device_id_type=MESH,
+        )
+        for i, (a, b, p) in enumerate([(to_next, from_last, after), (to_last, from_next, before)])
+    ]
+    for e in edges:
+        e.start()
+    start3(1, n // 4)
+    wait1()
+    if forward:
+        piece[...] = got[source[0]]
+    else:
+        total = lax.fori_loop(
+            0, n, lambda i, t: t + got[i].astype(F32), jnp.zeros(piece.shape, F32)
+        )
+        piece[...] = total.astype(BF16)
+    start2()
+    start3(n // 4)
+    wait2()
+    for e in edges:
+        e.wait()
+    wait3()
+    if forward:
+        wait_heads()
+
+
+def trade(source, parts, blocks, to_next, to_last, queries=()):
+    n = lax.axis_size("ctx")
+    hn = lax.axis_size("head") if queries else 0
+    dma = pltpu.SemaphoreType.DMA
+    outs = [jax.ShapeDtypeStruct(a.shape, BF16) for a in (parts, blocks, to_next, to_last)]
+    if queries:
+        rows, cols = queries[0].shape
+        outs.append(jax.ShapeDtypeStruct((2, rows * hn, cols // hn), BF16))
+    return pl.pallas_call(
+        functools.partial(trade_kernel, n, hn),
+        out_shape=outs,
+        in_specs=[SMEM, VMEM] + [ANY] * (3 + len(queries)),
+        out_specs=[ANY] * len(outs),
+        scratch_shapes=[
+            pltpu.VMEM(parts.shape, BF16),
+            pltpu.VMEM(parts.shape[1:], BF16),
+            *[dma((n,))] * 6,
+            dma((2,)),
+            dma((2,)),
+            dma((3,)),
+            *(head_sems(hn) if queries else []),
+        ],
+        compiler_params=pltpu.CompilerParams(
+            collective_id=1 if queries else 2, has_side_effects=True
+        ),
+    )(source, parts, blocks, to_next, to_last, *queries)
 
 
 def per_device(queries, key_states, value_states, out_grad, random_blocks, global_blocks):
     kv = to_heads(key_states, value_states)
-    qg = to_heads(queries, out_grad)
     tokens, cols = kv.shape[1:]
     blocks = tokens // BS
     devices = lax.axis_size("ctx")
     me = lax.axis_index("ctx")
     entries = blocks * NR
-    up = [(i, i + 1) for i in range(devices - 1)]
-    down = [(j, i) for i, j in up]
     kv = kv.reshape(2, blocks, BS, cols)
 
     table = random_blocks.reshape(devices, entries)
@@ -184,13 +371,16 @@
     ).astype(jnp.int32)
 
     rows = NG * 2 * BS // devices
-    pieces = exchange(pick(kv, global_offset).reshape(devices, rows, cols))
-    source = jnp.take(global_owner, me * NG // devices)
-    piece = lax.dynamic_index_in_dim(pieces, source, 0, keepdims=True)
-    glob = exchange(jnp.broadcast_to(piece, (devices, rows, cols))).reshape(NG, 2, BS, cols)
-    incoming = exchange(pick(kv, served_block))
-    before = lax.ppermute(kv[:, blocks - 1], "ctx", up)
-    after = lax.ppermute(kv[:, 0], "ctx", down)
+    source = jnp.take(global_owner, me * NG // devices).reshape(1)
+    glob, incoming, before, after, qg = trade(
+        source,
+        pick(kv, global_offset).reshape(devices, rows, cols),
+        pick(kv, served_block),
+        kv[:, blocks - 1],
+        kv[:, 0],
+        (queries, out_grad),
+    )
+    glob = glob.reshape(NG, 2, BS, cols)
 
     width = 2 * DH if cols % (2 * DH) == 0 else DH
     shape = jax.ShapeDtypeStruct
@@ -209,12 +399,10 @@
         width,
     )
 
-    far_parts = exchange(far.reshape(devices, rows, cols))
-    far_piece = jnp.sum(far_parts.astype(F32), axis=0, keepdims=True).astype(BF16)
-    arrived = exchange(back)
-    far_sum = exchange(jnp.broadcast_to(far_piece, (devices, rows, cols))).reshape(NG, 2, BS, cols)
-    from_next = lax.ppermute(rim_a, "ctx", down)
-    from_last = lax.ppermute(rim_b, "ctx", up)
+    far_sum, arrived, from_last, from_next = trade(
+        source, far.reshape(devices, rows, cols), back, rim_b, rim_a
+    )
+    far_sum = far_sum.reshape(NG, 2, BS, cols)
     dk, dv = by_columns(
         functools.partial(finish_kernel, blocks, devices),
         finish_scalars,

time: 424 us -> 398 us (0.939); the launches traced: 423 us -> 392 us
  Pallas kernels: 57.2 us -> 370 us
  waiting for transfers between devices: 227 us -> 0 us
  blocking collectives: 58.8 us -> 0 us
  starting transfers between devices: 42.1 us -> 0 us
  local copies, waits for them, and re-layouts: 32.8 us -> 17.6 us
    pallas_call x0 -> x3, Pallas kernels: none -> 315 us  [the longest x2 297 us: trade(): pl.pallas_call(functools.partial(trade_kernel, n, hn), out_shape=outs, in...]
    ppermute x4 -> x0, waiting for transfers between devices: 170 us -> none  [the longest x1 88 us: per_device(): from_last = lax.ppermute(rim_b, 'ctx', up)]
    all_to_all x2 -> x0, blocking collectives: 58.8 us -> none  [exchange(): return lax.all_to_all(x, 'ctx', split_axis=0, concat_axis=0, tiled=True)]
    all_to_all x6 -> x0, waiting for transfers between devices: 57 us -> none  [the longest x4 33.1 us: exchange(): return lax.all_to_all(x, 'ctx', split_axis=0, concat_axis=0, tiled=True)]
    all_to_all x6 -> x0, starting transfers between devices: 30.4 us -> none  [the longest x4 23.2 us: exchange(): return lax.all_to_all(x, 'ctx', split_axis=0, concat_axis=0, tiled=True)]
    ppermute x4 -> x0, starting transfers between devices: 11.7 us -> none  [the longest x1 4.19 us: per_device(): before = lax.ppermute(kv[:, blocks - 1], 'ctx', up)]
    all_to_all x2 -> x0, local copies, waits for them, and re-layouts: 8.25 us -> none  [to_heads(): lax.all_to_all(jnp.stack([x, y]), 'head', split_axis=2, concat_axis=1, ti...]
    another operation x3 -> x1, local copies, waits for them, and re-layouts: 6.27 us -> 0.61 us  [per_device(): source = jnp.take(global_owner, me * NG // devices).reshape(1)]
  transfers between devices with their start and end apart: 10 -> 0, of which waited for: 7 -> 0; matrix products, arithmetic and copies ran while one was open for 4% -> 0% of each run, Pallas kernels for 2% -> 0%
where the time goes in v2:
time: 398 us; the launch traced here: 392 us
  Pallas kernels  370 us (93%)
  local copies, waits for them, and re-layouts  17.6 us (4%)
    pallas_call x2, Pallas kernels, trade(): pl.pallas_call(functools.partial(trade_kernel, n, hn), out_shape=outs, in...  297 us
    pallas_call x2, Pallas kernels, by_columns(): pl.pallas_call(kernel, out_shape=outs, grid_spec=pltpu.PrefetchScalarGrid...  40.3 us
    pallas_call x1, Pallas kernels, to_heads(): pl.pallas_call(functools.partial(heads_kernel, n), out_shape=jax.ShapeDty...  18.3 us
    unnamed x29, local copies, waits for them, and re-layouts  14.8 us
    pallas_call x2, Pallas kernels, pick(): pl.pallas_call(pick_kernel, out_shape=jax.ShapeDtypeStruct((n, 2, BS, col...  14.6 us

profile of v2, /device:TPU:13, one launch (start us, length us, event | category | flops | bytes accessed | tf_op | source)
XLA Modules:
  0.0 392.4 jit_solution(306121747793041398)
XLA Ops:
  0.7 0.7 fusion.4
  1.4 0.7 fusion.2
  2.1 1.2 compare_select_fusion
  3.3 0.6 dynamic-slice.2
  4.6 0.1 reduce_or.14
  4.6 0.1 reduce_or.18
  4.8 0.1 reduce_sum.14
  4.8 0.1 reduce_sum.18.idx_ref
  5.0 0.0 copy-start.13
  5.0 0.1 pad_add_fusion.1.sc
  5.1 0.8 copy.9
  5.9 0.1 reshape.30
  5.9 0.1 pad_add_fusion.sc
  6.0 18.3 %shard_map.85 = bf16[2,128,2048]{2,1,0:T(8,128)(2,1)} custom-call(bf16[64,4096]{1,0:T(8,128)(2,1)} %x.1, bf16[64,4096]{1,0:T(8,128)(2,1)} %y.1), custom_call_target="tpu_custom_call" | custom-call | tf_op jit(solution)/shard_map/pallas_call | solution.py:233
  24.3 1.9 slice_bitcast_fusion
  26.2 4.0 %shard_map.86 = bf16[4,2,32,2048]{3,2,1,0:T(8,128)(2,1)} custom-call(s32[4]{0:T(128)} %get-tuple-element.51.idx_ref, bf16[2,4,32,2048]{3,2,1,0:T(8,128)(2,1)} %bitcast.21), custom_call_target="tpu_custom_call" | custom-call | tf_op jit(solution)/shard_map/pallas_call | solution.py:29
  30.2 0.0 copy-done.13
  30.2 10.6 %shard_map.87.blocks = bf16[16,2,32,2048]{3,2,1,0:T(8,128)(2,1)} custom-call(s32[16]{0:T(128)} %copy-done.13, bf16[2,4,32,2048]{3,2,1,0:T(8,128)(2,1)} %bitcast.22), custom_call_target="tpu_custom_call" | custom-call | tf_op jit(solution)/shard_map/pallas_call | solution.py:29
  40.8 0.0 copy-start
  40.8 147.7 %shard_map.88 = (bf16[16,16,2048]{2,1,0:T(8,128)(2,1)}, bf16[16,2,32,2048]{3,2,1,0:T(8,128)(2,1)}, bf16[2,32,2048]{2,1,0:T(8,128)(2,1)}, bf16[2,32,2048]{2,1,0:T(8,128)(2,1)}, bf16[2,128,2048]{2,1,0:T(8,128)(2,1)}) custom-call(s32[1]{0:T(128)S(6)} %select_n.81.source, bf16[16,16,2048]{2,1,0:T(8,128)(2,1)} %bitcast.27, ...), custom_call_target="tpu_custom_call" | custom-call | tf_op jit(solution)/shard_map/pallas_call | solution.py:328
  188.5 0.0 copy-done
  188.5 0.0 copy-start.3
  188.5 1.2 copy-done.3
  189.7 0.0 copy-start.4
  189.7 1.2 copy-done.4
  190.9 0.0 copy-start.9
  190.9 0.9 copy-done.9
  191.9 0.0 copy-start.10
  191.9 0.9 copy-done.10
  192.8 35.2 %shard_map.89 = (bf16[128,2048]{1,0:T(8,128)(2,1)}, bf16[16,2,32,2048]{3,2,1,0:T(8,128)(2,1)S(1)}, bf16[4,2,32,2048]{3,2,1,0:T(8,128)(2,1)S(1)}, f32[2,4,32,2048...) custom-call(s32[14]{0:T(128)S(1)} %pad_add_fusion.sc, ...), custom_call_target="tpu_custom_call" | custom-call | tf_op jit(solution)/shard_map/pallas_call | solution.py:136
  228.0 0.0 copy-start.1
  228.0 1.9 copy-done.1
  230.0 0.0 copy-start.6
  230.0 1.1 copy-done.6
  231.0 0.0 copy-start.7
  231.0 0.7 copy-done.7
  231.7 0.0 copy-start.8
  231.8 0.7 copy-done.8
  232.5 149.5 %shard_map.90 = (bf16[16,16,2048]{2,1,0:T(8,128)(2,1)}, bf16[16,2,32,2048]{3,2,1,0:T(8,128)(2,1)}, bf16[2,32,2048]{2,1,0:T(8,128)(2,1)}, bf16[2,32,2048]{2,1,0:T(8,128)(2,1)}) custom-call(s32[1]{0:T(128)S(6)} %select_n.81.source, bf16[16,16,2048]{2,1,0:T(8,128)(2,1)} %bitcast.26, bf16[16,2,32,2048]{3,2,1,0:T(8,128)(2,1)} %copy-done.1, ...), custom_call_target="tpu_custom_call" | custom-call | tf_op jit(solution)/shard_map/pallas_call | solution.py:328
  382.0 0.0 copy-start.2
  382.0 2.2 copy-done.2
  384.2 0.0 copy-start.5
  384.2 1.2 copy-done.5
  385.4 0.0 copy-start.11
  385.4 0.9 copy-done.11
  386.4 0.0 copy-start.12
  386.4 0.9 copy-done.12
  387.3 5.0 %shard_map.91 = (bf16[128,2048]{1,0:T(8,128)(2,1)}, bf16[128,2048]{1,0:T(8,128)(2,1)}) custom-call(s32[20]{0:T(128)S(1)} %pad_add_fusion.1.sc, f32[2,4,32,2048]{3,2,1,0:T(8,128)S(1)} %get-tuple-element.26.own, bf16[16,2,32,2048]{3,2,1,0:T(8,128)(2,1)S(1)} %copy-done.2, bf16[4,2,32,2048]{3,2,1,0:T(8,128)(2,1)S(1)} %bitcast.25, ...), custom_call_target="tpu_custom_call" | custom-call | tf_op jit(solution)/shard_map/pallas_call | solution.py:136
  (2 shorter events, 0.0 us)
Async XLA Ops:
  5.0 25.2 %copy-start.13 = (s32[16]{0:T(128)}, s32[16]{0:T(128)S(1)}, u32[]{:S(2)}) copy-start(s32[16]{0:T(128)S(1)} %reduce_sum.18.idx_ref) | copy-start | bytes 196
  40.8 147.7 %copy-start = (bf16[2,128,2048]{2,1,0:T(8,128)(2,1)S(1)}, bf16[2,128,2048]{2,1,0:T(8,128)(2,1)}, u32[]{:S(2)}) copy-start(bf16[2,128,2048]{2,1,0:T(8,128)(2,1)} %shard_map.85) | copy-start | bytes 3145732
  188.5 1.2 copy-start.3
  189.7 1.2 copy-start.4
  190.9 0.9 copy-start.9
  191.9 0.9 copy-start.10
  228.0 1.9 copy-start.1
  230.0 1.1 copy-start.6
  231.0 0.7 copy-start.7
  231.7 0.7 copy-start.8
  382.0 2.2 copy-start.2
  384.2 1.2 copy-start.5
  385.4 0.9 copy-start.11
  386.4 0.9 copy-start.12

commit v3 on v2

--- a/solution.py
+++ b/solution.py
@@ -20,34 +20,16 @@
     return lax.dot_general(a, b, (dims, ((), ())), preferred_element_type=F32)
 
 
-def pick_kernel(idx_ref, x_ref, o_ref):
-    o_ref[0] = x_ref[:, 0]
-
-
-def pick(kv, idx):
-    n, cols = idx.shape[0], kv.shape[3]
-    return pl.pallas_call(
-        pick_kernel,
-        out_shape=jax.ShapeDtypeStruct((n, 2, BS, cols), BF16),
-        grid_spec=pltpu.PrefetchScalarGridSpec(
-            num_scalar_prefetch=1,
-            grid=(n,),
-            in_specs=[pl.BlockSpec((2, 1, BS, cols), lambda r, idx: (0, idx[r], 0, 0))],
-            out_specs=pl.BlockSpec((1, 2, BS, cols), lambda r, idx: (r, 0, 0, 0)),
-        ),
-    )(idx, kv)
-
-
 def attend_kernel(
-    blocks, heads, sc, qg, kv, before, after, incoming, glob, dq, back, far, own, rim_a, rim_b
+    blocks, heads, sc, qg, kv, dq, back, far, own, rim_a, rim_b
 ):
     inv_root = 1.0 / math.sqrt(DH)
     entries = blocks * NR
     for h in range(heads):
         c = slice(h * DH, (h + 1) * DH)
         back[:, :, :, c] = jnp.zeros((back.shape[0], 2, BS, DH), BF16)
-        gk = [glob[i, 0, :, c] for i in range(NG)]
-        gv = [glob[i, 1, :, c] for i in range(NG)]
+        gk, gv = ([kv[w, sc[2 * entries + 3 + i], :, c] for i in range(NG)] for w in range(2))
+        first, final = sc[2 * entries + 2], kv.shape[1] - 1
         totals = [[None] * blocks, [None] * blocks]
         far_total = [None, None]
 
@@ -60,12 +42,9 @@
             qn, gn = qg[0, rows, c], qg[1, rows, c]
 
             def listed(w, far_list):
-                out = [
-                    before[w, :, c] if n == 0 else kv[w, n - 1, :, c],
-                    kv[w, n, :, c],
-                    after[w, :, c] if n == blocks - 1 else kv[w, n + 1, :, c],
-                ]
-                out += [incoming[sc[n * NR + j], w, :, c] for j in range(NR)]
+                at = [jnp.maximum(first + n - 1, 0), first + n, jnp.minimum(first + n + 1, final)]
+                at += [sc[entries + 2 + n * NR + j] for j in range(NR)]
+                out = [kv[w, m, :, c] for m in at]
                 return jnp.concatenate(out + far_list, axis=0)
 
             kn, vn = listed(0, gk), listed(1, gv)
@@ -214,11 +193,6 @@
     return wait
 
 
-def heads_kernel(n, x, y, out, send, recv, local):
-    meet([("head", n)])
-    head_exchange(n, (x, y), out, send, recv, local)()
-
-
 def head_sems(n):
     return [
         pltpu.SemaphoreType.DMA((2, n)),
@@ -227,17 +201,129 @@
     ]
 
 
-def to_heads(x, y):
-    n = lax.axis_size("head")
-    rows, cols = x.shape
+def grid_of(n):
+    return (n // 4, 2, 2) if n == 16 else (n // 4, 4, 1)
+
+
+def gather_kernel(n, hn, k, v, q, g, kv, qg, send, recv, *sems):
+    nz, ny, nc = grid_of(n)
+    me = lax.axis_index("ctx")
+    z, y, c = me // (ny * nc), (me // nc) % ny, me % nc
+
+    def at(z, y, c):
+        return (z * ny + y) * nc + c
+
+    def copy(w, shard, peer, way):
+        return pltpu.make_async_remote_copy(
+            src_ref=kv.at[w, shard],
+            dst_ref=kv.at[w, shard],
+            send_sem=send.at[w, shard, way],
+            recv_sem=recv.at[w, shard],
+            device_id={"ctx": peer},
+            device_id_type=MESH,
+        )
+
+    def across(w, shard):
+        return [copy(w, shard, at(z, lax.rem(y + d, ny), c), 1 + d) for d in range(1, ny)]
+
+    def inside(w, shard):
+        return [copy(w, shard, at(z, y, lax.rem(c + d, nc)), 1 + ny - 1 + d) for d in range(1, nc)]
+
+    def along(w, shard, up):
+        return copy(w, shard, at(z + 1 if up else z - 1, y, c), 0 if up else 1)
+
+    def has_next(up):
+        return z + 1 < nz if up else z > 0
+
+    def every_send(do):
+        for dist in range(nz):
+            for up in (True, False):
+                far = z - dist if up else z + dist
+
+                @pl.when((far >= 0) if up else (far < nz))
+                def _():
+                    for d in range(ny):
+                        yy = lax.rem(y + d, ny)
+                        shard = at(far, yy, c)
+                        if d == 0:
+                            do(0, shard, dist, up, True, up or dist > 0)
+                        do(1, shard, dist, up, False, up or dist > 0, d)
+
+            for up in (True, False):
+                far = z - dist if up else z + dist
+                if dist == 0 and not up:
+                    continue
+
+                @pl.when((far >= 0) if up else (far < nz))
+                def _():
+                    for d in range(1, ny):
+                        do(0, at(far, lax.rem(y + d, ny), c), dist, None, False, True, d)
+
+    def start(w, shard, dist, up, cross, once, d=0):
+        if once and (dist > 0 or d > 0):
+            copy(w, shard, at(z, y, c), 0).wait_recv()
+        if up is not None:
+
+            @pl.when(has_next(up))
+            def _():
+                along(w, shard, up).start()
+
+        if once:
+            own_line = w == 0 and cross
+            own_shard = w == 1 and dist == 0 and d == 0
+            for e in (across(w, shard) if own_line or own_shard else []) + inside(w, shard):
+                e.start()
+
+    def finish(w, shard, dist, up, cross, once, d=0):
+        if up is not None:
+
+            @pl.when(has_next(up))
+            def _():
+                along(w, shard, up).wait_send()
+
+        if once:
+            own_line = w == 0 and cross
+            own_shard = w == 1 and dist == 0 and d == 0
+            for e in (across(w, shard) if own_line or own_shard else []) + inside(w, shard):
+                e.wait_send()
+
+    meet([("ctx", n), ("head", hn)])
+    head_exchange(hn, (k, v), kv.at[:, me], *sems[:3])()
+    wait_heads = head_exchange(hn, (q, g), qg, *sems[3:])
+    every_send(start)
+    for d in range(1, nc):
+        cc = lax.rem(c + d, nc)
+
+        def arrive(i, carry):
+            for w in range(2):
+                copy(w, i * nc + cc, at(z, y, c), 0).wait_recv()
+            return carry
+
+        lax.fori_loop(0, nz * ny, arrive, 0)
+    every_send(finish)
+    wait_heads()
+
+
+def gather(k, v, q, g):
+    n, hn = lax.axis_size("ctx"), lax.axis_size("head")
+    _, ny, nc = grid_of(n)
+    rows, cols = k.shape[0] * hn, k.shape[1] // hn
     return pl.pallas_call(
-        functools.partial(heads_kernel, n),
-        out_shape=jax.ShapeDtypeStruct((2, rows * n, cols // n), BF16),
-        in_specs=[ANY, ANY],
-        out_specs=ANY,
-        scratch_shapes=head_sems(n),
+        functools.partial(gather_kernel, n, hn),
+        out_shape=[
+            jax.ShapeDtypeStruct((2, n, rows, cols), BF16),
+            jax.ShapeDtypeStruct((2, rows, cols), BF16),
+        ],
+        in_specs=[ANY] * 4,
+        out_specs=[ANY] * 2,
+        scratch_shapes=[
+            pltpu.SemaphoreType.DMA((2, n, ny + nc)),
+            pltpu.SemaphoreType.DMA((2, n)),
+            *head_sems(hn),
+            *head_sems(hn),
+        ],
         compiler_params=pltpu.CompilerParams(collective_id=0, has_side_effects=True),
-    )(x, y)
+    )(k, v, q, g)
 
 
 def all_to_all(n, src, dst, send, recv, local):
@@ -267,24 +353,16 @@
     return start, wait
 
 
-def trade_kernel(n, hn, source, parts, blocks, to_next, to_last, *refs):
-    forward = hn > 0
-    if forward:
-        q, g, parts_out, blocks_out, from_last, from_next, qg = refs[:7]
-        refs = refs[7:]
-    else:
-        parts_out, blocks_out, from_last, from_next = refs[:4]
-        refs = refs[4:]
-    got, piece, s1, r1, s2, r2, s3, r3, s4, r4, local = refs[:11]
+def trade_kernel(n, parts, blocks, to_next, to_last, *refs):
+    parts_out, blocks_out, from_last, from_next = refs[:4]
+    got, piece, s1, r1, s2, r2, s3, r3, s4, r4, local = refs[4:]
     me = lax.axis_index("ctx")
     after, before = lax.rem(me + 1, n), lax.rem(me + n - 1, n)
-    meet([("ctx", n)] + ([("head", hn)] if forward else []))
+    meet([("ctx", n)])
     start1, wait1 = all_to_all(n, lambda p: parts.at[p], got, s1, r1, local.at[0])
     start2, wait2 = all_to_all(n, lambda p: piece, parts_out, s2, r2, local.at[1])
     start3, wait3 = all_to_all(n, lambda p: blocks.at[p], blocks_out, s3, r3, local.at[2])
     start1()
-    if forward:
-        wait_heads = head_exchange(hn, (q, g), qg, *refs[11:])
     edges = [
         pltpu.make_async_remote_copy(
             src_ref=a,
@@ -300,36 +378,24 @@
         e.start()
     start3(1, n // 4)
     wait1()
-    if forward:
-        piece[...] = got[source[0]]
-    else:
-        total = lax.fori_loop(
-            0, n, lambda i, t: t + got[i].astype(F32), jnp.zeros(piece.shape, F32)
-        )
-        piece[...] = total.astype(BF16)
+    total = lax.fori_loop(0, n, lambda i, t: t + got[i].astype(F32), jnp.zeros(piece.shape, F32))
+    piece[...] = total.astype(BF16)
     start2()
     start3(n // 4)
     wait2()
     for e in edges:
         e.wait()
     wait3()
-    if forward:
-        wait_heads()
-
-
-def trade(source, parts, blocks, to_next, to_last, queries=()):
+
+
+def trade(parts, blocks, to_next, to_last):
     n = lax.axis_size("ctx")
-    hn = lax.axis_size("head") if queries else 0
     dma = pltpu.SemaphoreType.DMA
-    outs = [jax.ShapeDtypeStruct(a.shape, BF16) for a in (parts, blocks, to_next, to_last)]
-    if queries:
-        rows, cols = queries[0].shape
-        outs.append(jax.ShapeDtypeStruct((2, rows * hn, cols // hn), BF16))
     return pl.pallas_call(
-        functools.partial(trade_kernel, n, hn),
-        out_shape=outs,
-        in_specs=[SMEM, VMEM] + [ANY] * (3 + len(queries)),
-        out_specs=[ANY] * len(outs),
+        functools.partial(trade_kernel, n),
+        out_shape=[jax.ShapeDtypeStruct(a.shape, BF16) for a in (parts, blocks, to_next, to_last)],
+        in_specs=[VMEM] + [ANY] * 3,
+        out_specs=[ANY] * 4,
         scratch_shapes=[
             pltpu.VMEM(parts.shape, BF16),
             pltpu.VMEM(parts.shape[1:], BF16),
@@ -337,32 +403,31 @@
             dma((2,)),
             dma((2,)),
             dma((3,)),
-            *(head_sems(hn) if queries else []),
         ],
-        compiler_params=pltpu.CompilerParams(
-            collective_id=1 if queries else 2, has_side_effects=True
-        ),
-    )(source, parts, blocks, to_next, to_last, *queries)
+        compiler_params=pltpu.CompilerParams(collective_id=1, has_side_effects=True),
+    )(parts, blocks, to_next, to_last)
 
 
 def per_device(queries, key_states, value_states, out_grad, random_blocks, global_blocks):
-    kv = to_heads(key_states, value_states)
-    tokens, cols = kv.shape[1:]
+    kv, qg = gather(key_states, value_states, queries, out_grad)
+    tokens, cols = kv.shape[2:]
     blocks = tokens // BS
     devices = lax.axis_size("ctx")
     me = lax.axis_index("ctx")
     entries = blocks * NR
-    kv = kv.reshape(2, blocks, BS, cols)
+    kv = kv.reshape(2, devices * blocks, BS, cols)
 
     table = random_blocks.reshape(devices, entries)
     served = table // blocks == me
     served_block = jnp.sum(jnp.where(served, table % blocks, 0), axis=1)
     served_used = jnp.any(served, axis=1)
-    my_owner = lax.dynamic_index_in_dim(table, me, 0, keepdims=False) // blocks
+    mine = lax.dynamic_index_in_dim(table, me, 0, keepdims=False)
     global_owner = global_blocks // blocks
     global_offset = global_blocks % blocks
     edge = jnp.stack([jnp.where(me == 0, BS, 0), jnp.where(me == devices - 1, BS, 0)])
-    attend_scalars = jnp.concatenate([my_owner, edge]).astype(jnp.int32)
+    attend_scalars = jnp.concatenate(
+        [mine // blocks, edge, mine, (me * blocks)[None], global_blocks]
+    ).astype(jnp.int32)
     finish_scalars = jnp.concatenate(
         [
             jnp.where(served_used, served_block, blocks),
@@ -371,23 +436,12 @@
     ).astype(jnp.int32)
 
     rows = NG * 2 * BS // devices
-    source = jnp.take(global_owner, me * NG // devices).reshape(1)
-    glob, incoming, before, after, qg = trade(
-        source,
-        pick(kv, global_offset).reshape(devices, rows, cols),
-        pick(kv, served_block),
-        kv[:, blocks - 1],
-        kv[:, 0],
-        (queries, out_grad),
-    )
-    glob = glob.reshape(NG, 2, BS, cols)
-
     width = 2 * DH if cols % (2 * DH) == 0 else DH
     shape = jax.ShapeDtypeStruct
     dq, back, far, own, rim_a, rim_b = by_columns(
         functools.partial(attend_kernel, blocks, width // DH),
         attend_scalars,
-        [qg, kv, before, after, incoming, glob],
+        [qg, kv],
         [
             shape((tokens, cols), BF16),
             shape((devices, 2, BS, cols), BF16),
@@ -400,7 +454,7 @@
     )
 
     far_sum, arrived, from_last, from_next = trade(
-        source, far.reshape(devices, rows, cols), back, rim_b, rim_a
+        far.reshape(devices, rows, cols), back, rim_b, rim_a
     )
     far_sum = far_sum.reshape(NG, 2, BS, cols)
     dk, dv = by_columns(

time: 398 us -> 358 us (0.90)
  Pallas kernels: 370 us -> 339 us
  local copies, waits for them, and re-layouts: 17.6 us -> 12.7 us
    pallas_call x5 -> x2, Pallas kernels: 330 us -> 299 us  [the longest x1 151 us: trade(): pl.pallas_call(functools.partial(trade_kernel, n), out_shape=[jax.ShapeDt...]
    unnamed x29 -> x19, local copies, waits for them, and re-layouts: 14.8 us -> 11.7 us
where the time goes in v3:
time: 358 us; the launch traced here: 354 us
  Pallas kernels  339 us (95%)
  local copies, waits for them, and re-layouts  12.7 us (4%)
    pallas_call x1, Pallas kernels, trade(): pl.pallas_call(functools.partial(trade_kernel, n), out_shape=[jax.ShapeDt...  151 us
    pallas_call x1, Pallas kernels, gather(): pl.pallas_call(functools.partial(gather_kernel, n, hn), out_shape=[jax.Sh...  147 us
    pallas_call x2, Pallas kernels, by_columns(): pl.pallas_call(kernel, out_shape=outs, grid_spec=pltpu.PrefetchScalarGrid...  40.5 us
    unnamed x19, local copies, waits for them, and re-layouts  11.7 us

profile of v3, /device:TPU:13, one launch (start us, length us, event | category | flops | bytes accessed | tf_op | source)
XLA Modules:
  0.0 354.3 jit_solution(15917391051428805877)
XLA Ops:
  0.6 0.7 compare_select_fusion
  1.3 0.7 fusion.2
  2.0 0.1 reduce_or.14
  2.1 0.1 reduce_or.18
  2.3 0.1 reduce_sum.14
  2.3 0.1 reduce_sum.18
  2.5 0.1 pad_add_fusion.sc
  2.6 0.8 copy.9
  3.3 0.1 reshape.20
  3.4 0.7 concatenate.6.sc
  4.2 147.2 %shard_map.85 = (bf16[2,16,128,2048]{3,2,1,0:T(8,128)(2,1)}, bf16[2,128,2048]{2,1,0:T(8,128)(2,1)}) custom-call(bf16[64,4096]{1,0:T(8,128)(2,1)} %k.1, bf16[64,4096]{1,0:T(8,128)(2,1)} %v.1, bf16[64,4096]{1,0:T(8,128)(2,1)} %q.1, bf16[64,4096]{1,0:T(8,128)(2,1)} %g.1), custom_call_target="tpu_custom_call" | custom-call | tf_op jit(solution)/shard_map/pallas_call | solution.py:311
  151.4 0.0 copy-start.3
  151.4 1.2 copy-done.3
  152.6 35.4 %shard_map.86 = (bf16[128,2048]{1,0:T(8,128)(2,1)}, bf16[16,2,32,2048]{3,2,1,0:T(8,128)(2,1)S(1)}, bf16[4,2,32,2048]{3,2,1,0:T(8,128)(2,1)S(1)}, f32[2,4,32,2048...) custom-call(s32[31]{0:T(128)S(1)} %concatenate.6.sc, ...), custom_call_target="tpu_custom_call" | custom-call | tf_op jit(solution)/shard_map/pallas_call | solution.py:115
  188.0 0.0 copy-start
  188.0 1.9 copy-done
  190.0 0.0 copy-start.4
  190.0 1.0 copy-done.4
  191.0 0.0 copy-start.5
  191.0 0.7 copy-done.5
  191.7 0.0 copy-start.6
  191.7 0.7 copy-done.6
  192.4 151.4 %shard_map.87 = (bf16[16,16,2048]{2,1,0:T(8,128)(2,1)}, bf16[16,2,32,2048]{3,2,1,0:T(8,128)(2,1)}, bf16[2,32,2048]{2,1,0:T(8,128)(2,1)}, bf16[2,32,2048]{2,1,0:T(8,128)(2,1)}) custom-call(bf16[16,16,2048]{2,1,0:T(8,128)(2,1)} %bitcast.10, bf16[16,2,32,2048]{3,2,1,0:T(8,128)(2,1)} %copy-done, bf16[2,32,2048]{2,1,0:T(8,128)(2,1)} %copy-done.6, ...), custom_call_target="tpu_custom_call" | custom-call | tf_op jit(solution)/shard_map/pallas_call | solution.py:394
  343.8 0.0 copy-start.1
  343.8 2.2 copy-done.1
  346.0 0.0 copy-start.2
  346.0 1.2 copy-done.2
  347.2 0.0 copy-start.7
  347.2 0.9 copy-done.7
  348.2 0.0 copy-start.8
  348.2 0.9 copy-done.8
  349.1 5.2 %shard_map.88 = (bf16[128,2048]{1,0:T(8,128)(2,1)}, bf16[128,2048]{1,0:T(8,128)(2,1)}) custom-call(s32[20]{0:T(128)S(1)} %pad_add_fusion.sc, f32[2,4,32,2048]{3,2,1,0:T(8,128)S(1)} %get-tuple-element.20.own, bf16[16,2,32,2048]{3,2,1,0:T(8,128)(2,1)S(1)} %copy-done.1, bf16[4,2,32,2048]{3,2,1,0:T(8,128)(2,1)S(1)} %bitcast.9, ...), custom_call_target="tpu_custom_call" | custom-call | tf_op jit(solution)/shard_map/pallas_call | solution.py:115
  (3 shorter events, 0.0 us)
Async XLA Ops:
  151.4 1.2 copy-start.3
  188.0 1.9 copy-start
  190.0 1.1 copy-start.4
  191.0 0.7 copy-start.5
  191.7 0.7 copy-start.6
  343.8 2.2 copy-start.1
  346.0 1.2 copy-start.2
  347.2 0.9 copy-start.7
  348.2 0.9 copy-start.8

commit v4 on v3

--- a/solution.py
+++ b/solution.py
@@ -32,6 +32,7 @@
         first, final = sc[2 * entries + 2], kv.shape[1] - 1
         totals = [[None] * blocks, [None] * blocks]
         far_total = [None, None]
+        staged, ready = [], []
 
         def add(which, m, part):
             old = totals[which][m]
@@ -57,11 +58,17 @@
                 if n == blocks - 1:
                     bad = (col >= 2 * BS) & (col < 2 * BS + sc[entries + 1])
                     s = jnp.where(bad, -jnp.inf, s)
+            staged.append((rows, qn, gn, kn, s, dp))
+
+        for n, (rows, qn, gn, kn, s, dp) in enumerate(staged):
             e = jnp.exp(s - jnp.max(s, axis=1, keepdims=True))
             p = e / jnp.sum(e, axis=1, keepdims=True)
             ph = p.astype(BF16)
             row_dot = jnp.sum(ph.astype(F32) * dp, axis=1, keepdims=True)
             ds = (p * (dp - row_dot)).astype(BF16)
+            ready.append((rows, qn, gn, kn, ph, ds))
+
+        for n, (rows, qn, gn, kn, ph, ds) in enumerate(ready):
             dq[rows, c] = (dot(ds, kn, ((1,), (0,))) * inv_root).astype(BF16)
             for w, part in (
                 (0, dot(ds, qn, ((0,), (0,))) * inv_root),
@@ -376,12 +383,12 @@
     ]
     for e in edges:
         e.start()
-    start3(1, n // 4)
+    start3(1, n // 2)
     wait1()
     total = lax.fori_loop(0, n, lambda i, t: t + got[i].astype(F32), jnp.zeros(piece.shape, F32))
     piece[...] = total.astype(BF16)
     start2()
-    start3(n // 4)
+    start3(n // 2)
     wait2()
     for e in edges:
         e.wait()

time: 358 us -> 335 us (0.936); the launches traced: 354 us -> 335 us
  Pallas kernels: 339 us -> 320 us
    pallas_call x2, Pallas kernels: 40.5 us -> 23.1 us  [by_columns(): pl.pallas_call(kernel, out_shape=outs, grid_spec=pltpu.PrefetchScalarGrid...]
where the time goes in v4:
time: 335 us
  Pallas kernels  320 us (96%)
  local copies, waits for them, and re-layouts  12.7 us (4%)
    pallas_call x1, Pallas kernels, trade(): pl.pallas_call(functools.partial(trade_kernel, n), out_shape=[jax.ShapeDt...  149 us
    pallas_call x1, Pallas kernels, gather(): pl.pallas_call(functools.partial(gather_kernel, n, hn), out_shape=[jax.Sh...  147 us
    pallas_call x2, Pallas kernels, by_columns(): pl.pallas_call(kernel, out_shape=outs, grid_spec=pltpu.PrefetchScalarGrid...  23.1 us
    unnamed x19, local copies, waits for them, and re-layouts  11.7 us

profile of v4, /device:TPU:13, one launch (start us, length us, event | category | flops | bytes accessed | tf_op | source)
XLA Modules:
  0.0 334.9 jit_solution(9874781469600086340)
XLA Ops:
  0.6 0.7 compare_select_fusion
  1.3 0.7 fusion.2
  2.0 0.1 reduce_or.14
  2.1 0.1 reduce_or.18
  2.3 0.1 reduce_sum.14
  2.3 0.1 reduce_sum.18
  2.5 0.1 pad_add_fusion.sc
  2.6 0.8 copy.9
  3.3 0.1 reshape.20
  3.4 0.7 concatenate.6.sc
  4.2 147.2 %shard_map.85 = (bf16[2,16,128,2048]{3,2,1,0:T(8,128)(2,1)}, bf16[2,128,2048]{2,1,0:T(8,128)(2,1)}) custom-call(bf16[64,4096]{1,0:T(8,128)(2,1)} %k.1, bf16[64,4096]{1,0:T(8,128)(2,1)} %v.1, bf16[64,4096]{1,0:T(8,128)(2,1)} %q.1, bf16[64,4096]{1,0:T(8,128)(2,1)} %g.1), custom_call_target="tpu_custom_call" | custom-call | tf_op jit(solution)/shard_map/pallas_call | solution.py:318
  151.4 0.0 copy-start.3
  151.4 1.2 copy-done.3
  152.6 18.0 %shard_map.86 = (bf16[128,2048]{1,0:T(8,128)(2,1)}, bf16[16,2,32,2048]{3,2,1,0:T(8,128)(2,1)S(1)}, bf16[4,2,32,2048]{3,2,1,0:T(8,128)(2,1)S(1)}, f32[2,4,32,2048...) custom-call(s32[31]{0:T(128)S(1)} %concatenate.6.sc, ...), custom_call_target="tpu_custom_call" | custom-call | tf_op jit(solution)/shard_map/pallas_call | solution.py:122
  170.7 0.0 copy-start
  170.7 1.9 copy-done
  172.6 0.0 copy-start.4
  172.6 1.0 copy-done.4
  173.7 0.0 copy-start.5
  173.7 0.7 copy-done.5
  174.4 0.0 copy-start.6
  174.4 0.7 copy-done.6
  175.1 149.5 %shard_map.87 = (bf16[16,16,2048]{2,1,0:T(8,128)(2,1)}, bf16[16,2,32,2048]{3,2,1,0:T(8,128)(2,1)}, bf16[2,32,2048]{2,1,0:T(8,128)(2,1)}, bf16[2,32,2048]{2,1,0:T(8,128)(2,1)}) custom-call(bf16[16,16,2048]{2,1,0:T(8,128)(2,1)} %bitcast.10, bf16[16,2,32,2048]{3,2,1,0:T(8,128)(2,1)} %copy-done, bf16[2,32,2048]{2,1,0:T(8,128)(2,1)} %copy-done.6, ...), custom_call_target="tpu_custom_call" | custom-call | tf_op jit(solution)/shard_map/pallas_call | solution.py:401
  324.5 0.0 copy-start.1
  324.5 2.2 copy-done.1
  326.7 0.0 copy-start.2
  326.7 1.2 copy-done.2
  328.0 0.0 copy-start.7
  328.0 0.9 copy-done.7
  328.9 0.0 copy-start.8
  328.9 0.9 copy-done.8
  329.9 5.0 %shard_map.88 = (bf16[128,2048]{1,0:T(8,128)(2,1)}, bf16[128,2048]{1,0:T(8,128)(2,1)}) custom-call(s32[20]{0:T(128)S(1)} %pad_add_fusion.sc, f32[2,4,32,2048]{3,2,1,0:T(8,128)S(1)} %get-tuple-element.20.own, bf16[16,2,32,2048]{3,2,1,0:T(8,128)(2,1)S(1)} %copy-done.1, bf16[4,2,32,2048]{3,2,1,0:T(8,128)(2,1)S(1)} %bitcast.9, ...), custom_call_target="tpu_custom_call" | custom-call | tf_op jit(solution)/shard_map/pallas_call | solution.py:122
  (3 shorter events, 0.0 us)
Async XLA Ops:
  151.4 1.2 copy-start.3
  170.7 1.9 copy-start
  172.6 1.1 copy-start.4
  173.7 0.7 copy-start.5
  174.4 0.7 copy-start.6
  324.5 2.2 copy-start.1
  326.7 1.2 copy-start.2
  328.0 0.9 copy-start.7
  328.9 0.9 copy-start.8

commit v5 on v4

--- a/solution.py
+++ b/solution.py
@@ -383,12 +383,13 @@
     ]
     for e in edges:
         e.start()
-    start3(1, n // 2)
+    start3(n // 4, n - n // 4)
     wait1()
     total = lax.fori_loop(0, n, lambda i, t: t + got[i].astype(F32), jnp.zeros(piece.shape, F32))
     piece[...] = total.astype(BF16)
     start2()
-    start3(n // 2)
+    start3(1, n // 4)
+    start3(n - n // 4)
     wait2()
     for e in edges:
         e.wait()

time: 335 us -> 335 us (level)
  no operation moved by 1% of the time
where the time goes in v5:
time: 335 us
  Pallas kernels  320 us (96%)
  local copies, waits for them, and re-layouts  12.7 us (4%)
    pallas_call x1, Pallas kernels, trade(): pl.pallas_call(functools.partial(trade_kernel, n), out_shape=[jax.ShapeDt...  149 us
    pallas_call x1, Pallas kernels, gather(): pl.pallas_call(functools.partial(gather_kernel, n, hn), out_shape=[jax.Sh...  147 us
    pallas_call x2, Pallas kernels, by_columns(): pl.pallas_call(kernel, out_shape=outs, grid_spec=pltpu.PrefetchScalarGrid...  23.2 us
    unnamed x19, local copies, waits for them, and re-layouts  11.7 us

profile of v5, /device:TPU:13, one launch (start us, length us, event | category | flops | bytes accessed | tf_op | source)
XLA Modules:
  0.0 334.9 jit_solution(756948455961583482)
XLA Ops:
  0.6 0.7 compare_select_fusion
  1.3 0.7 fusion.2
  2.0 0.1 reduce_or.14
  2.1 0.1 reduce_or.18
  2.3 0.1 reduce_sum.14
  2.3 0.1 reduce_sum.18
  2.5 0.1 pad_add_fusion.sc
  2.6 0.8 copy.9
  3.3 0.1 reshape.20
  3.4 0.7 concatenate.6.sc
  4.2 147.2 %shard_map.85 = (bf16[2,16,128,2048]{3,2,1,0:T(8,128)(2,1)}, bf16[2,128,2048]{2,1,0:T(8,128)(2,1)}) custom-call(bf16[64,4096]{1,0:T(8,128)(2,1)} %k.1, bf16[64,4096]{1,0:T(8,128)(2,1)} %v.1, bf16[64,4096]{1,0:T(8,128)(2,1)} %q.1, bf16[64,4096]{1,0:T(8,128)(2,1)} %g.1), custom_call_target="tpu_custom_call" | custom-call | tf_op jit(solution)/shard_map/pallas_call | solution.py:318
  151.4 0.0 copy-start.3
  151.4 1.2 copy-done.3
  152.6 18.0 %shard_map.86 = (bf16[128,2048]{1,0:T(8,128)(2,1)}, bf16[16,2,32,2048]{3,2,1,0:T(8,128)(2,1)S(1)}, bf16[4,2,32,2048]{3,2,1,0:T(8,128)(2,1)S(1)}, f32[2,4,32,2048...) custom-call(s32[31]{0:T(128)S(1)} %concatenate.6.sc, ...), custom_call_target="tpu_custom_call" | custom-call | tf_op jit(solution)/shard_map/pallas_call | solution.py:122
  170.7 0.0 copy-start
  170.7 1.9 copy-done
  172.6 0.0 copy-start.4
  172.6 1.0 copy-done.4
  173.7 0.0 copy-start.5
  173.7 0.7 copy-done.5
  174.4 0.0 copy-start.6
  174.4 0.7 copy-done.6
  175.1 149.4 %shard_map.87 = (bf16[16,16,2048]{2,1,0:T(8,128)(2,1)}, bf16[16,2,32,2048]{3,2,1,0:T(8,128)(2,1)}, bf16[2,32,2048]{2,1,0:T(8,128)(2,1)}, bf16[2,32,2048]{2,1,0:T(8,128)(2,1)}) custom-call(bf16[16,16,2048]{2,1,0:T(8,128)(2,1)} %bitcast.10, bf16[16,2,32,2048]{3,2,1,0:T(8,128)(2,1)} %copy-done, bf16[2,32,2048]{2,1,0:T(8,128)(2,1)} %copy-done.6, ...), custom_call_target="tpu_custom_call" | custom-call | tf_op jit(solution)/shard_map/pallas_call | solution.py:402
  324.5 0.0 copy-start.1
  324.5 2.2 copy-done.1
  326.7 0.0 copy-start.2
  326.7 1.2 copy-done.2
  327.9 0.0 copy-start.7
  327.9 0.9 copy-done.7
  328.9 0.0 copy-start.8
  328.9 0.9 copy-done.8
  329.8 5.1 %shard_map.88 = (bf16[128,2048]{1,0:T(8,128)(2,1)}, bf16[128,2048]{1,0:T(8,128)(2,1)}) custom-call(s32[20]{0:T(128)S(1)} %pad_add_fusion.sc, f32[2,4,32,2048]{3,2,1,0:T(8,128)S(1)} %get-tuple-element.20.own, bf16[16,2,32,2048]{3,2,1,0:T(8,128)(2,1)S(1)} %copy-done.1, bf16[4,2,32,2048]{3,2,1,0:T(8,128)(2,1)S(1)} %bitcast.9, ...), custom_call_target="tpu_custom_call" | custom-call | tf_op jit(solution)/shard_map/pallas_call | solution.py:122
  (3 shorter events, 0.0 us)
Async XLA Ops:
  151.4 1.2 copy-start.3
  170.7 1.9 copy-start
  172.6 1.1 copy-start.4
  173.7 0.7 copy-start.5
  174.4 0.7 copy-start.6
  324.5 2.2 copy-start.1
  326.7 1.2 copy-start.2
  327.9 0.9 copy-start.7
  328.9 0.9 copy-start.8
